TPU v7x, 512 devices: a whole 4x8x8 slice. The times are simulated.
512 devices in a mesh: ctx: 32 (over x_lo, y, core), nar: 16 (over x_hi, z).
Axes of the slice: x: 4 (x_hi: 2, x_lo: 2; x = x_hi * 2 + x_lo), y: 8, z: 8, core: 2. Of those that a mesh axis runs over, the one named last changes fastest.
Arguments:
- q_proj: bfloat16 [64, 262144], P(None, ('ctx', 'nar')), may hold values from -6 to 6
- k_proj: bfloat16 [64, 262144], P(None, ('ctx', 'nar')), may hold values from -6 to 6
- v_proj: bfloat16 [64, 262144], P(None, ('ctx', 'nar')), may hold values from -6 to 6
- skip_gain: float32 [64], replicated, may hold values from -1 to 1
- spectrum: float32 [2, 2, 64, 262144], P(None, None, None, ('ctx', 'nar')), may hold values from -6 to 6
Outputs:
- gated_output: bfloat16 [64, 262144], P(None, ('ctx', 'nar'))
All inputs are finite; a program needn't handle non-finite values.
Results may differ from a plain program's by a relative error of at most 0.0025.
Values sent between devices are 32-bit elements; how exact they have to be, the bound alone decides.
No kernel may reach another device: no remote copies, remote signals or barrier semaphores. Data moves between devices by JAX's collectives and lax.ppermute only.
A program may use at most 64 MiB of HBM per device.

v0:
```python
import math

import jax
import jax.numpy as jnp
import ml_dtypes
import numpy as np
from jax import lax
from jax.experimental import pallas as pl
from jax.experimental.pallas import tpu as pltpu
from jax.sharding import PartitionSpec as P

G = 32
H = 16
T = 512
LANES = 128
CHUNKS = T // LANES
ROWS = 2 * CHUNKS
FULL = 2 * G * H * T
VMEM_LIMIT = 24 * 1024 * 1024


def bit_reverse(value, bits):
    out = 0
    for place in range(bits):
        out |= (value >> place & 1) << (bits - 1 - place)
    return out


def block_freqs(j):
    first = [0, 32] if j == 0 else [j, 64 - j]
    return first + [16 + j, 48 - j]


def add(a, b):
    if a is None:
        return b
    return a if b is None else a + b


def sub(a, b):
    if b is None:
        return a
    return -b if a is None else a - b


def twist(value, steps, period):
    re, im = value
    eighth = 8 * steps % (8 * period)
    if eighth == 0:
        return value
    if eighth == 2 * period:
        return -im, re
    if eighth == 4 * period:
        return -re, -im
    if eighth == 6 * period:
        return im, -re
    c = math.cos(2 * math.pi * steps / period)
    s = math.sin(2 * math.pi * steps / period)
    if abs(abs(c) - abs(s)) < 1e-12:
        r = math.sqrt(0.5)
        cs, ss = math.copysign(1.0, c), math.copysign(1.0, s)
        a = re if cs > 0 else -re
        b = im if cs > 0 else -im
        return (
            ((a - im) if ss > 0 else (a + im)) * r,
            ((b + re) if ss > 0 else (b - re)) * r,
        )
    return re * c - im * s, re * s + im * c


def real_forward(x):
    n = len(x)
    if n == 2:
        return [(add(x[0], x[1]), None), (sub(x[0], x[1]), None)]
    even, odd = real_forward(x[0::2]), real_forward(x[1::2])
    out = [None] * (n // 2 + 1)
    out[0] = (even[0][0] + odd[0][0], None)
    out[n // 2] = (even[0][0] - odd[0][0], None)
    out[n // 4] = (even[n // 4][0], -odd[n // 4][0])
    for k in range(1, n // 4):
        tr, ti = twist(odd[k], -k, n)
        er, ei = even[k]
        out[k] = (er + tr, ei + ti)
        out[n // 2 - k] = (er - tr, ti - ei)
    return out


def real_inverse(x):
    n = 2 * (len(x) - 1)
    if n == 2:
        return [x[0][0] + x[1][0]]
    even, odd = [None] * (n // 4 + 1), [None] * (n // 4 + 1)
    even[0] = (x[0][0] + x[n // 2][0], None)
    odd[0] = (x[0][0] - x[n // 2][0], None)
    even[n // 4] = (2.0 * x[n // 4][0], None)
    odd[n // 4] = (-2.0 * x[n // 4][1], None)
    for k in range(1, n // 4):
        ar, ai = x[k]
        br, bi = x[n // 2 - k]
        even[k] = (ar + br, ai - bi)
        odd[k] = twist((ar - br, ai + bi), k, n)
    out = [None] * (n // 2)
    out[0::2], out[1::2] = real_inverse(even), real_inverse(odd)
    return out


def complex_transform(x, sign):
    n = len(x)
    if n == 1:
        return x
    even, odd = complex_transform(x[0::2], sign), complex_transform(x[1::2], sign)
    low, high = [], []
    for k in range(n // 2):
        tr, ti = twist(odd[k], sign * k, n)
        er, ei = even[k]
        low.append((er + tr, ei + ti))
        high.append((er - tr, ei - ti))
    return low + high


def times(a, b):
    return a[0] * b[0] - a[1] * b[1], a[0] * b[1] + a[1] * b[0]


def times_conj(a, b):
    return a[0] * b[0] + a[1] * b[1], a[1] * b[0] - a[0] * b[1]


SEND_A = 5 * ROWS
SEND_B = 12 * ROWS
SEND_C = 4 * ROWS


def pack_kernel(k_ref, v_ref, spec_ref, out_ref):
    product = k_ref[...].astype(jnp.float32) * v_ref[...].astype(jnp.float32)
    for half in range(2):
        rows = slice(half * G, half * G + G)
        for chunk in range(CHUNKS):
            cols = slice(chunk * LANES, (chunk + 1) * LANES)
            place = half * CHUNKS + chunk
            out_ref[pl.ds(place, G, stride=SEND_A), :] = product[rows, cols]
            for part in range(4):
                out_ref[pl.ds((part + 1) * ROWS + place, G, stride=SEND_A), :] = spec_ref[
                    part, rows, cols
                ]


def coarse_kernel(in_ref, out_ref):
    tokens = [in_ref[pl.ds(g * SEND_A, ROWS), :] for g in range(G)]
    freqs = real_forward(tokens + [None] * G)
    items = [(freqs[0][0], freqs[32][0])] + freqs[1:32]
    for j in range(H):
        base = j * SEND_B
        for e in range(2):
            for part in range(2):
                out_ref[pl.ds(base + (2 * e + part) * ROWS, ROWS), :] = items[j + 16 * e][part]
        for slot, q in enumerate(block_freqs(j)):
            source = bit_reverse(q >> 1, 5) * SEND_A + (1 + 2 * (q & 1)) * ROWS
            out_ref[pl.ds(base + (4 + 2 * slot) * ROWS, 2 * ROWS), :] = in_ref[
                pl.ds(source, 2 * ROWS), :
            ]


def split(value):
    high = value.astype(jnp.bfloat16)
    return high, (value - high.astype(jnp.float32)).astype(jnp.bfloat16)


def dense(high_ref, low_ref, table_high, table_low):
    def dot(a, b):
        return jnp.dot(a[...], b[...], preferred_element_type=jnp.float32)

    return dot(high_ref, table_high) + (dot(low_ref, table_high) + dot(high_ref, table_low))


def filter_kernel(
    j_ref, step_ref, in_ref, slow_ref, fast_ref, high_ref, low_ref, out_ref,
    re_ref, im_ref, turn_ref, xh_ref, xl_ref,
):
    j = j_ref[0]
    packed = j == 0
    for e in range(2):
        pairs = [[], []]
        for h in range(H):
            re = in_ref[pl.ds(h * SEND_B + 2 * e * ROWS, ROWS), :]
            im = in_ref[pl.ds(h * SEND_B + (2 * e + 1) * ROWS, ROWS), :]
            if e == 0:
                zero = jnp.zeros_like(im)
                pairs[0].append((re, jnp.where(packed, zero, im)))
                pairs[1].append((jnp.where(packed, im, re), jnp.where(packed, zero, -im)))
            else:
                pairs[0].append((re, im))
                pairs[1].append((re, -im))
        for side in range(2):
            slot = 2 * e + side
            turned = []
            for h in range(H):
                at = ((j * 4 + slot) * H + h) * 2
                turned.append(times(pairs[side][h], (step_ref[at], step_ref[at + 1])))
            slow = (slow_ref[j, slot, 0], slow_ref[j, slot, 1])
            for kh, value in enumerate(complex_transform(turned, -1)):
                turn = times(slow, (fast_ref[kh, 0], fast_ref[kh, 1]))
                at = slot * H + kh
                turn_ref[at, 0], turn_ref[at, 1] = turn
                re_ref[pl.ds(at * ROWS, ROWS), :], im_ref[pl.ds(at * ROWS, ROWS), :] = times(
                    value, turn
                )
    half_rows = 4 * 2 * H
    for block in range(8):
        slot, ch = block // 2, block % 2
        for part, ref in enumerate((re_ref, im_ref)):
            rows = slice(part * half_rows + block * H, part * half_rows + (block + 1) * H)
            for chunk in range(CHUNKS):
                cols = slice(chunk * LANES, (chunk + 1) * LANES)
                start = slot * H * ROWS + ch * CHUNKS + chunk
                high, low = split(ref[pl.ds(start, H, stride=ROWS), :])
                xh_ref[rows, cols] = high
                xl_ref[rows, cols] = low
    mixed = dense(xh_ref, xl_ref, high_ref, low_ref)
    for block in range(8):
        slot, ch = block // 2, block % 2
        top = slice(block * H, (block + 1) * H)
        bottom = slice(half_rows + block * H, half_rows + (block + 1) * H)
        for chunk in range(CHUNKS):
            cols = slice(chunk * LANES, (chunk + 1) * LANES)
            sine_cols = slice(T + chunk * LANES, T + (chunk + 1) * LANES)
            value = (
                mixed[top, cols] + mixed[bottom, sine_cols],
                mixed[bottom, cols] - mixed[top, sine_cols],
            )
            start = (4 + 2 * slot) * ROWS + ch * CHUNKS + chunk
            response = (
                in_ref[pl.ds(start, H, stride=SEND_B), :],
                in_ref[pl.ds(start + ROWS, H, stride=SEND_B), :],
            )
            filtered = times(value, response)
            for rows, part in ((top, 0), (bottom, 1)):
                high, low = split(filtered[part])
                xh_ref[rows, cols] = high
                xl_ref[rows, cols] = low
    mixed = dense(xh_ref, xl_ref, high_ref, low_ref)
    for block in range(8):
        slot, ch = block // 2, block % 2
        top = slice(block * H, (block + 1) * H)
        bottom = slice(half_rows + block * H, half_rows + (block + 1) * H)
        for chunk in range(CHUNKS):
            cols = slice(chunk * LANES, (chunk + 1) * LANES)
            sine_cols = slice(T + chunk * LANES, T + (chunk + 1) * LANES)
            start = slot * H * ROWS + ch * CHUNKS + chunk
            re_ref[pl.ds(start, H, stride=ROWS), :] = mixed[top, cols] - mixed[bottom, sine_cols]
            im_ref[pl.ds(start, H, stride=ROWS), :] = mixed[bottom, cols] + mixed[top, sine_cols]
    for e in range(2):
        sides = []
        for side in range(2):
            slot = 2 * e + side
            values = []
            for kh in range(H):
                at = slot * H + kh
                value = (re_ref[pl.ds(at * ROWS, ROWS), :], im_ref[pl.ds(at * ROWS, ROWS), :])
                values.append(times_conj(value, (turn_ref[at, 0], turn_ref[at, 1])))
            values = complex_transform(values, 1)
            for h in range(H):
                at = ((j * 4 + slot) * H + h) * 2
                values[h] = times_conj(values[h], (step_ref[at], step_ref[at + 1]))
            sides.append(values)
        for h in range(H):
            (ar, ai), (br, bi) = sides[0][h], sides[1][h]
            re, im = (ar + br) * (0.5 / FULL), (ai - bi) * (0.5 / FULL)
            if e == 0:
                re = jnp.where(packed, ar * (1.0 / FULL), re)
                im = jnp.where(packed, br * (1.0 / FULL), im)
            out_ref[pl.ds(h * SEND_C + 2 * e * ROWS, ROWS), :] = re
            out_ref[pl.ds(h * SEND_C + (2 * e + 1) * ROWS, ROWS), :] = im


def uncoarse_kernel(in_ref, out_ref):
    def item(i):
        base = i % 16 * SEND_C + i // 16 * 2 * ROWS
        return in_ref[pl.ds(base, ROWS), :], in_ref[pl.ds(base + ROWS, ROWS), :]

    first = item(0)
    freqs = [(first[0], None)] + [item(i) for i in range(1, 32)] + [(first[1], None)]
    for g, value in enumerate(real_inverse(freqs)):
        out_ref[pl.ds(g * ROWS, ROWS), :] = value


def gate_kernel(in_ref, q_ref, k_ref, v_ref, gain_ref, out_ref):
    channels = q_ref.shape[0]
    row = lax.broadcasted_iota(jnp.int32, (channels, channels), 0)
    col = lax.broadcasted_iota(jnp.int32, (channels, channels), 1)
    spread = jnp.broadcast_to(gain_ref[...], (channels, channels))
    gain = jnp.sum(jnp.where(row == col, spread, 0.0), axis=1, keepdims=True)
    product = k_ref[...].astype(jnp.float32) * v_ref[...].astype(jnp.float32)
    convolved = jnp.concatenate(
        [
            jnp.concatenate(
                [
                    in_ref[pl.ds(half * CHUNKS + chunk, G, stride=ROWS), :]
                    for chunk in range(CHUNKS)
                ],
                axis=1,
            )
            for half in range(2)
        ],
        axis=0,
    )
    gated = q_ref[...].astype(jnp.float32) * (convolved + gain * product)
    out_ref[...] = gated.astype(jnp.bfloat16)


def split_table(table):
    high = table.astype(np.float32).astype(ml_dtypes.bfloat16)
    low = (table - high.astype(np.float64)).astype(np.float32).astype(ml_dtypes.bfloat16)
    return high, low


def tables():
    t = np.arange(T)
    angle = 2 * np.pi * (t[:, None] * t[None, :] % T) / T
    high, low = split_table(np.concatenate([np.cos(angle), np.sin(angle)], axis=1))
    freqs = np.array([block_freqs(j) for j in range(H)])
    step = 2 * np.pi * (freqs[:, :, None] * np.arange(H) % (2 * G * H)) / (2 * G * H)
    step = np.stack([np.cos(step), -np.sin(step)], axis=-1).reshape(-1).astype(np.float32)

    def rows_of(angles):
        pair = np.stack([np.cos(angles), -np.sin(angles)], axis=-2)
        pair = pair.reshape(pair.shape[:-1] + (CHUNKS, LANES))
        return np.concatenate([pair, pair], axis=-2).astype(np.float32)

    slow = rows_of(2 * np.pi * (freqs[:, :, None] * t % FULL) / FULL)
    fast = rows_of(2 * np.pi * (np.arange(H)[:, None] * t % (H * T)) / (H * T))
    return high, low, step, slow, fast


def call(kernel, shape, in_specs=None, dtype=jnp.float32, scratch=()):
    extra = {} if in_specs is None else {"in_specs": in_specs}
    return pl.pallas_call(
        kernel,
        out_shape=jax.ShapeDtypeStruct(shape, dtype),
        scratch_shapes=list(scratch),
        compiler_params=pltpu.CompilerParams(vmem_limit_bytes=VMEM_LIMIT),
        **extra,
    )


def exchange(value, axis, count):
    blocks = value.reshape(count, -1, LANES)
    return lax.all_to_all(blocks, axis, 0, 0, tiled=True).reshape(-1, LANES)


VMEM = pl.BlockSpec(memory_space=pltpu.VMEM)
SMEM = pl.BlockSpec(memory_space=pltpu.SMEM)


def run_filter(position, value):
    high, low, step, slow, fast = tables()
    rows = 4 * H * ROWS
    return call(
        filter_kernel,
        (H * SEND_C, LANES),
        in_specs=[SMEM, SMEM] + [VMEM] * 5,
        scratch=[
            pltpu.VMEM((rows, LANES), jnp.float32),
            pltpu.VMEM((rows, LANES), jnp.float32),
            pltpu.VMEM((4 * H, 2, ROWS, LANES), jnp.float32),
            pltpu.VMEM((16 * H, T), jnp.bfloat16),
            pltpu.VMEM((16 * H, T), jnp.bfloat16),
        ],
    )(position, step, value, slow, fast, high, low)


def local(q_proj, k_proj, v_proj, skip_gain, spectrum):
    channels, tokens = q_proj.shape
    value = call(pack_kernel, (G * SEND_A, LANES))(
        k_proj, v_proj, spectrum.reshape(4, channels, tokens)
    )
    value = exchange(value, "ctx", G)
    value = call(coarse_kernel, (H * SEND_B, LANES))(value)
    value = exchange(value, "nar", H)
    value = run_filter(lax.axis_index("nar").astype(jnp.int32).reshape(1), value)
    value = exchange(value, "nar", H)
    value = call(uncoarse_kernel, (G * ROWS, LANES))(value)
    value = exchange(value, "ctx", G)
    return call(gate_kernel, (channels, tokens), dtype=jnp.bfloat16)(
        value, q_proj, k_proj, v_proj, skip_gain.reshape(1, channels)
    )


def solution(mesh):
    placed = (
        P(None, ("ctx", "nar")),
        P(None, ("ctx", "nar")),
        P(None, ("ctx", "nar")),
        P(),
        P(None, None, None, ("ctx", "nar")),
    )
    return jax.shard_map(
        local, mesh=mesh, in_specs=placed, out_specs=P(None, ("ctx", "nar")), check_vma=False
    )
```

profile of v0, /device:TPU:1, one launch (start us, length us, event | category | flops | bytes accessed | tf_op | source)
XLA Modules:
  0.0 103.1 jit_solution(1811525189292990243)
XLA Ops:
  0.0 1.0 %copy-done.2 = f32[2,2,64,512]{3,2,1,0:T(8,128)S(1)} copy-done((f32[2,2,64,512]{3,2,1,0:T(8,128)S(1)}, f32[2,2,64,512]{3,2,1,0:T(8,128)}, u32[]{:S(2)}) %copy-start.2) | copy-done | bytes 524312
  1.0 0.8 copy-done.4
  1.9 0.8 copy-done.6
  2.7 0.1 shard_map.100
  2.9 28.7 %all_to_all.20 = f32[32,40,128]{2,1,0:T(8,128)S(1)} all-to-all(f32[32,40,128]{2,1,0:T(8,128)S(1)} %bitcast.13), channel_id=1, replica_groups=mesh['ctx'=32,'nar'=16] {'ctx'}, dimensions={0} | all-to-all | bytes 1310720 | tf_op jit(solution)/shard_map/all_to_all | solution.py:348
  31.5 1.0 shard_map.101
  32.5 12.3 %all-to-all-start.1 = ((f32[16,96,128]{2,1,0:T(8,128)}), f32[16,96,128]{2,1,0:T(8,128)S(1)}, u32[]{:S(2)}, u32[]{:S(2)}) async-start(f32[16,96,128]{2,1,0:T(8,128)} %bitcast.4), calls=%async_computation.1 | async-start | bytes 1572864 | tf_op jit(solution)/shard_map/all_to_all | solution.py:348
  44.8 0.0 copy-start.10
  44.8 19.0 %all-to-all-done.1 = f32[16,96,128]{2,1,0:T(8,128)S(1)} async-done(((f32[16,96,128]{2,1,0:T(8,128)}), f32[16,96,128]{2,1,0:T(8,128)S(1)}, u32[]{:S(2)}, u32[]{:S(2)}) %all-to-all-start.1) | async-done | bytes 786464 | tf_op jit(solution)/shard_map/all_to_all | solution.py:348
  63.9 0.0 copy-done.1
  63.9 0.0 copy-done.8
  63.9 0.0 copy-done
  63.9 0.0 copy-done.3
  63.9 0.0 copy-done.10
  63.9 3.6 %shard_map.102 = f32[512,128]{1,0:T(8,128)S(1)} custom-call(s32[1]{0:T(128)} %bitcast.j_ref, f32[2048]{0:T(1024)S(1)} %copy-done.10, f32[1536,128]{1,0:T(8,128)S(1)} %bitcast.11, f32[16,4,2,8,128]{4,3,2,1,0:T(8,128)S(1)} %copy-done.3, f32[16,2,8,128]{3,2,1,0:T(8,128)S(1)} %copy-done.8, bf16[512,1024]{1,0:T(8,128)(2,1)S(1)} %copy-done, ...), custom_call_target="tpu_custom_call" | custom-call | tf_op jit(solution)/shard_map/pallas_call | solution.py:358
  67.5 16.0 %all_to_all.21 = f32[16,32,128]{2,1,0:T(8,128)S(1)} all-to-all(f32[16,32,128]{2,1,0:T(8,128)S(1)} %bitcast.14), channel_id=1, replica_groups=mesh['ctx'=32,'nar'=16] {'nar'}, dimensions={0} | all-to-all | bytes 524288 | tf_op jit(solution)/shard_map/all_to_all | solution.py:348
  83.5 0.1 shard_map.103
  83.6 0.0 copy-start.5
  83.6 0.0 copy-start.7
  83.6 0.0 copy-start.9
  83.6 18.1 %all_to_all.22 = f32[32,8,128]{2,1,0:T(8,128)S(1)} all-to-all(f32[32,8,128]{2,1,0:T(8,128)S(1)} %bitcast.16), channel_id=1, replica_groups=mesh['ctx'=32,'nar'=16] {'ctx'}, dimensions={0} | all-to-all | bytes 262144 | tf_op jit(solution)/shard_map/all_to_all | solution.py:348
  101.7 0.0 copy-done.7
  101.7 0.6 copy-done.11
  102.4 0.7 shard_map.104
  (10 shorter events, 0.0 us)
Async XLA Ops:
  0.0 1.0 %copy-start.2 = (f32[2,2,64,512]{3,2,1,0:T(8,128)S(1)}, f32[2,2,64,512]{3,2,1,0:T(8,128)}, u32[]{:S(2)}) copy-start(f32[2,2,64,512]{3,2,1,0:T(8,128)} %param.14) | copy-start | bytes 1572868
  1.0 0.8 copy-start.4
  1.9 0.8 copy-start.6
  31.5 32.3 %copy-start.1 = (bf16[512,1024]{1,0:T(8,128)(2,1)S(1)}, bf16[512,1024]{1,0:T(8,128)(2,1)}, u32[]{:S(2)}) copy-start(bf16[512,1024]{1,0:T(8,128)(2,1)} %constant.18.clone.low_ref) | copy-start | bytes 3145732
  31.5 32.3 %copy-start.8 = (f32[16,2,8,128]{3,2,1,0:T(8,128)S(1)}, f32[16,2,8,128]{3,2,1,0:T(8,128)}, u32[]{:S(2)}) copy-start(f32[16,2,8,128]{3,2,1,0:T(8,128)} %constant.16.clone.fast_ref) | copy-start | bytes 393220
  32.5 31.3 %copy-start = (bf16[512,1024]{1,0:T(8,128)(2,1)S(1)}, bf16[512,1024]{1,0:T(8,128)(2,1)}, u32[]{:S(2)}) copy-start(bf16[512,1024]{1,0:T(8,128)(2,1)} %constant.17.clone.high_ref) | copy-start | bytes 3145732
  32.5 31.3 %copy-start.3 = (f32[16,4,2,8,128]{4,3,2,1,0:T(8,128)S(1)}, f32[16,4,2,8,128]{4,3,2,1,0:T(8,128)}, u32[]{:S(2)}) copy-start(f32[16,4,2,8,128]{4,3,2,1,0:T(8,128)} %constant.15.clone.slow_ref) | copy-start | bytes 1572868
  32.5 31.3 %all-to-all-start.1 = ((f32[16,96,128]{2,1,0:T(8,128)}), f32[16,96,128]{2,1,0:T(8,128)S(1)}, u32[]{:S(2)}, u32[]{:S(2)}) async-start(f32[16,96,128]{2,1,0:T(8,128)} %bitcast.4), calls=%async_computation.1 | async-start | bytes 1572864 | tf_op jit(solution)/shard_map/all_to_all | solution.py:348
  44.8 19.1 %copy-start.10 = (f32[2048]{0:T(1024)S(1)}, f32[2048]{0:T(1024)}, u32[]{:S(2)}) copy-start(f32[2048]{0:T(1024)} %constant.14.clone.step_ref) | copy-start | bytes 24580
  83.6 18.1 %copy-start.5 = (bf16[64,512]{1,0:T(8,128)(2,1)S(1)}, bf16[64,512]{1,0:T(8,128)(2,1)}, u32[]{:S(2)}) copy-start(bf16[64,512]{1,0:T(8,128)(2,1)} %k_ref.3) | copy-start | bytes 196612
  83.6 18.1 %copy-start.7 = (bf16[64,512]{1,0:T(8,128)(2,1)S(1)}, bf16[64,512]{1,0:T(8,128)(2,1)}, u32[]{:S(2)}) copy-start(bf16[64,512]{1,0:T(8,128)(2,1)} %v_ref.3) | copy-start | bytes 196612
  83.6 18.1 %copy-start.9 = (bf16[64,512]{1,0:T(8,128)(2,1)S(1)}, bf16[64,512]{1,0:T(8,128)(2,1)}, u32[]{:S(2)}) copy-start(bf16[64,512]{1,0:T(8,128)(2,1)} %q_ref.1) | copy-start | bytes 196612
  101.7 0.7 copy-start.11
where the time goes:
time: 104 us; the launch traced here: 103 us
  blocking collectives  62.7 us (60%)
  waiting for transfers between devices  19 us (18%)
  starting transfers between devices  12.3 us (12%)
  Pallas kernels  5.63 us (5%)
  local copies, waits for them, and re-layouts  3.4 us (3%)
    all_to_all x3, blocking collectives, exchange(): return lax.all_to_all(blocks, axis, 0, 0, tiled=True).reshape(-1, LANES)  62.7 us
    all_to_all x1, waiting for transfers between devices, exchange(): return lax.all_to_all(blocks, axis, 0, 0, tiled=True).reshape(-1, LANES)  19 us
    all_to_all x1, starting transfers between devices, exchange(): return lax.all_to_all(blocks, axis, 0, 0, tiled=True).reshape(-1, LANES)  12.3 us
    pallas_call x1, Pallas kernels, run_filter(): call(filter_kernel, (H * SEND_C, LANES), in_specs=[SMEM, SMEM] + [VMEM] *...  3.64 us
    unnamed x24, local copies, waits for them, and re-layouts  3.4 us
  transfers between devices with their start and end apart: 1, of which 1 were waited for; matrix products, arithmetic and copies ran while one was open for 0% of the time, Pallas kernels for 0%

commit v1 on v0

v1 whole, which is shorter than its diff:
```python
import math

import jax
import jax.numpy as jnp
import ml_dtypes
import numpy as np
from jax import lax
from jax.experimental import pallas as pl
from jax.experimental.pallas import tpu as pltpu
from jax.sharding import Mesh, PartitionSpec as P

AXES = ("xl", "yh", "yl", "core", "xh", "zh", "zl")
SIZES = (2, 4, 2, 2, 2, 4, 2)
FAR = ("xl", "yh", "zh")
NEAR = ("yl", "core", "xh", "zl")
A = 8
ZH = 4
N_FAR = A * ZH
N_NEAR = 16
D = 64
T = 512
LANES = 128
CHUNKS = T // LANES
ROWS = 2 * CHUNKS
FULL = 2 * A * D * T
VMEM_LIMIT = 24 * 1024 * 1024


def item_freqs(i):
    return (0, 8) if i == 0 else (i, 16 - i)


def source_of(q):
    xl, y2, y1 = q >> 1 & 1, q >> 2 & 1, q >> 3 & 1
    return q & 1, xl * 4 + y2 * 2 + y1


def digit(w, zh):
    return (w >> 1) * 8 + zh * 2 + (w & 1)


def freq_place(kd):
    y0, core, z0, z1, z2, xh = (kd >> bit & 1 for bit in range(6))
    return y0 * 8 + core * 4 + xh * 2 + z0, z2 * 2 + z1


def add(a, b):
    if a is None:
        return b
    return a if b is None else a + b


def sub(a, b):
    if b is None:
        return a
    return -b if a is None else a - b


def twist(value, steps, period):
    re, im = value
    eighth = 8 * steps % (8 * period)
    if eighth == 0:
        return value
    if eighth == 2 * period:
        return -im, re
    if eighth == 4 * period:
        return -re, -im
    if eighth == 6 * period:
        return im, -re
    c = math.cos(2 * math.pi * steps / period)
    s = math.sin(2 * math.pi * steps / period)
    if abs(abs(c) - abs(s)) < 1e-12:
        r = math.sqrt(0.5)
        cs, ss = math.copysign(1.0, c), math.copysign(1.0, s)
        a = re if cs > 0 else -re
        b = im if cs > 0 else -im
        return (
            ((a - im) if ss > 0 else (a + im)) * r,
            ((b + re) if ss > 0 else (b - re)) * r,
        )
    return re * c - im * s, re * s + im * c


def real_forward(x):
    n = len(x)
    if n == 2:
        return [(add(x[0], x[1]), None), (sub(x[0], x[1]), None)]
    even, odd = real_forward(x[0::2]), real_forward(x[1::2])
    out = [None] * (n // 2 + 1)
    out[0] = (even[0][0] + odd[0][0], None)
    out[n // 2] = (even[0][0] - odd[0][0], None)
    out[n // 4] = (even[n // 4][0], -odd[n // 4][0])
    for k in range(1, n // 4):
        tr, ti = twist(odd[k], -k, n)
        er, ei = even[k]
        out[k] = (er + tr, ei + ti)
        out[n // 2 - k] = (er - tr, ti - ei)
    return out


def real_inverse(x):
    n = 2 * (len(x) - 1)
    if n == 2:
        return [x[0][0] + x[1][0]]
    even, odd = [None] * (n // 4 + 1), [None] * (n // 4 + 1)
    even[0] = (x[0][0] + x[n // 2][0], None)
    odd[0] = (x[0][0] - x[n // 2][0], None)
    even[n // 4] = (2.0 * x[n // 4][0], None)
    odd[n // 4] = (-2.0 * x[n // 4][1], None)
    for k in range(1, n // 4):
        ar, ai = x[k]
        br, bi = x[n // 2 - k]
        even[k] = (ar + br, ai - bi)
        odd[k] = twist((ar - br, ai + bi), k, n)
    out = [None] * (n // 2)
    out[0::2], out[1::2] = real_inverse(even), real_inverse(odd)
    return out


def complex_transform(x, sign):
    n = len(x)
    if n == 1:
        return x
    even, odd = complex_transform(x[0::2], sign), complex_transform(x[1::2], sign)
    low, high = [], []
    for k in range(n // 2):
        tr, ti = twist(odd[k], sign * k, n)
        er, ei = even[k]
        low.append((er + tr, ei + ti))
        high.append((er - tr, ei - ti))
    return low + high


def times(a, b):
    return a[0] * b[0] - a[1] * b[1], a[0] * b[1] + a[1] * b[0]


def times_conj(a, b):
    return a[0] * b[0] + a[1] * b[1], a[1] * b[0] - a[0] * b[1]


SEND_A = 5 * ROWS
SEND_B = 12 * ROWS
SEND_C = 4 * ROWS


def pack_kernel(k_hbm, v_hbm, spec_hbm, out_ref, k_ref, v_ref, spec_ref, sems):
    copies = [
        pltpu.make_async_copy(source, target, sems.at[i])
        for i, (source, target) in enumerate(
            ((k_hbm, k_ref), (v_hbm, v_ref), (spec_hbm, spec_ref))
        )
    ]
    for copy in copies:
        copy.start()
    copies[0].wait()
    copies[1].wait()
    product = k_ref[...].astype(jnp.float32) * v_ref[...].astype(jnp.float32)
    for half in range(2):
        rows = slice(half * N_FAR, (half + 1) * N_FAR)
        for chunk in range(CHUNKS):
            cols = slice(chunk * LANES, (chunk + 1) * LANES)
            place = half * CHUNKS + chunk
            out_ref[pl.ds(place, N_FAR, stride=SEND_A), :] = product[rows, cols]
    copies[2].wait()
    for half in range(2):
        rows = slice(half * N_FAR, (half + 1) * N_FAR)
        for chunk in range(CHUNKS):
            cols = slice(chunk * LANES, (chunk + 1) * LANES)
            for parity in range(2):
                for part in range(2):
                    place = (1 + 2 * parity + half) * ROWS + part * CHUNKS + chunk
                    out_ref[pl.ds(place, N_FAR, stride=SEND_A), :] = spec_ref[
                        2 * parity + part, rows, cols
                    ]


def upper_rows():
    return lax.broadcasted_iota(jnp.int32, (ROWS, LANES), 0) < CHUNKS


def swap_halves(value):
    return pltpu.roll(value, CHUNKS, 0)


def regroup(first, second, upper):
    return (
        jnp.where(upper, first, swap_halves(second)),
        jnp.where(upper, swap_halves(first), second),
    )


def coarse_kernel(in_ref, out_ref):
    upper = upper_rows()
    for zh in range(ZH):
        tokens = [in_ref[pl.ds((a * ZH + zh) * SEND_A, ROWS), :] for a in range(A)]
        freqs = real_forward(tokens + [None] * A)
        items = [(freqs[0][0], freqs[A][0])] + freqs[1:A]
        for i in range(A):
            for ch, value in enumerate(regroup(items[i][0], items[i][1], upper)):
                base = (2 * i + ch) * SEND_B
                out_ref[pl.ds(base + zh * ROWS, ROWS), :] = value
                for side, q in enumerate(item_freqs(i)):
                    parity, a = source_of(q)
                    source = (a * ZH + zh) * SEND_A + (1 + 2 * parity + ch) * ROWS
                    target = base + (ZH + side * ZH + zh) * ROWS
                    out_ref[pl.ds(target, ROWS), :] = in_ref[pl.ds(source, ROWS), :]


def split(value):
    high = value.astype(jnp.bfloat16)
    return high, (value - high.astype(jnp.float32)).astype(jnp.bfloat16)


def dense(high_ref, low_ref, table_high, table_low):
    def dot(a, b):
        return jnp.dot(a[...], b[...], preferred_element_type=jnp.float32)

    return dot(high_ref, table_high) + (dot(low_ref, table_high) + dot(high_ref, table_low))


def filter_kernel(
    i_ref, in_ref, slow_ref, fast_ref, high_ref, low_ref, out_ref, re_ref, im_ref, xh_ref, xl_ref
):
    item = i_ref[0]
    packed = item == 0
    upper = upper_rows()
    keep = jnp.logical_or(upper, packed)
    signs = jnp.where(upper, 1.0, -1.0) * jnp.where(packed, 0.0, 1.0)
    values = [None] * D
    for w in range(N_NEAR):
        for zh in range(ZH):
            d = digit(w, zh)
            value = in_ref[pl.ds(w * SEND_B + zh * ROWS, ROWS), :]
            other = swap_halves(value)
            pair = (jnp.where(keep, value, other), jnp.where(upper, other, value) * signs)
            values[d] = times(pair, (slow_ref[item, d, 0], slow_ref[item, d, 1]))
    for kd, value in enumerate(complex_transform(values, -1)):
        w, zh = freq_place(kd)
        at = (zh * N_NEAR + w) * ROWS
        re_ref[pl.ds(at, ROWS), :], im_ref[pl.ds(at, ROWS), :] = times(
            value, (fast_ref[kd, 0], fast_ref[kd, 1])
        )
    half_rows = 2 * D
    blocks = []
    for side in range(2):
        for zh in range(ZH):
            first = (side * ZH + zh) * N_NEAR
            blocks.append(
                (
                    slice(first, first + N_NEAR),
                    slice(half_rows + first, half_rows + first + N_NEAR),
                    zh * N_NEAR * ROWS + side * CHUNKS,
                    (ZH + side * ZH + zh) * ROWS,
                )
            )
    for top, bottom, start, _ in blocks:
        for rows, ref in ((top, re_ref), (bottom, im_ref)):
            for chunk in range(CHUNKS):
                cols = slice(chunk * LANES, (chunk + 1) * LANES)
                high, low = split(ref[pl.ds(start + chunk, N_NEAR, stride=ROWS), :])
                xh_ref[rows, cols] = high
                xl_ref[rows, cols] = low
    mixed = dense(xh_ref, xl_ref, high_ref, low_ref)
    for top, bottom, _, start in blocks:
        for chunk in range(CHUNKS):
            cols = slice(chunk * LANES, (chunk + 1) * LANES)
            sine_cols = slice(T + chunk * LANES, T + (chunk + 1) * LANES)
            value = (
                mixed[top, cols] + mixed[bottom, sine_cols],
                mixed[bottom, cols] - mixed[top, sine_cols],
            )
            response = (
                in_ref[pl.ds(start + chunk, N_NEAR, stride=SEND_B), :],
                in_ref[pl.ds(start + CHUNKS + chunk, N_NEAR, stride=SEND_B), :],
            )
            for rows, part in zip((top, bottom), times(value, response)):
                high, low = split(part)
                xh_ref[rows, cols] = high
                xl_ref[rows, cols] = low
    mixed = dense(xh_ref, xl_ref, high_ref, low_ref)
    for top, bottom, start, _ in blocks:
        for chunk in range(CHUNKS):
            cols = slice(chunk * LANES, (chunk + 1) * LANES)
            sine_cols = slice(T + chunk * LANES, T + (chunk + 1) * LANES)
            place = pl.ds(start + chunk, N_NEAR, stride=ROWS)
            re_ref[place, :] = mixed[top, cols] - mixed[bottom, sine_cols]
            im_ref[place, :] = mixed[bottom, cols] + mixed[top, sine_cols]
    values = []
    for kd in range(D):
        w, zh = freq_place(kd)
        at = (zh * N_NEAR + w) * ROWS
        value = (re_ref[pl.ds(at, ROWS), :], im_ref[pl.ds(at, ROWS), :])
        values.append(times_conj(value, (fast_ref[kd, 0], fast_ref[kd, 1])))
    values = complex_transform(values, 1)
    scale = jnp.where(packed, 1.0 / FULL, 0.5 / FULL)
    for w in range(N_NEAR):
        for zh in range(ZH):
            d = digit(w, zh)
            re, im = times_conj(values[d], (slow_ref[item, d, 0], slow_ref[item, d, 1]))
            summed = jnp.where(upper, re + swap_halves(re), swap_halves(im) - im)
            out_ref[pl.ds(w * SEND_C + zh * ROWS, ROWS), :] = (
                jnp.where(packed, re, summed) * scale
            )


def uncoarse_kernel(in_ref, out_ref):
    upper = upper_rows()
    for zh in range(ZH):
        items = []
        for i in range(A):
            first = in_ref[pl.ds(2 * i * SEND_C + zh * ROWS, ROWS), :]
            second = in_ref[pl.ds((2 * i + 1) * SEND_C + zh * ROWS, ROWS), :]
            items.append(regroup(first, second, upper))
        freqs = [(items[0][0], None)] + items[1:] + [(items[0][1], None)]
        for a, value in enumerate(real_inverse(freqs)):
            out_ref[pl.ds((a * ZH + zh) * ROWS, ROWS), :] = value


def gate_kernel(in_ref, q_ref, k_ref, v_ref, gain_hbm, out_ref, gain_ref, sem):
    copy = pltpu.make_async_copy(gain_hbm, gain_ref, sem)
    copy.start()
    channels = q_ref.shape[0]
    row = lax.broadcasted_iota(jnp.int32, (channels, channels), 0)
    col = lax.broadcasted_iota(jnp.int32, (channels, channels), 1)
    product = k_ref[...].astype(jnp.float32) * v_ref[...].astype(jnp.float32)
    convolved = jnp.concatenate(
        [
            jnp.concatenate(
                [
                    in_ref[pl.ds(half * CHUNKS + chunk, N_FAR, stride=ROWS), :]
                    for chunk in range(CHUNKS)
                ],
                axis=1,
            )
            for half in range(2)
        ],
        axis=0,
    )
    copy.wait()
    spread = jnp.broadcast_to(gain_ref[...], (channels, channels))
    gain = jnp.sum(jnp.where(row == col, spread, 0.0), axis=1, keepdims=True)
    gated = q_ref[...].astype(jnp.float32) * (convolved + gain * product)
    out_ref[...] = gated.astype(jnp.bfloat16)


def split_table(table):
    high = table.astype(np.float32).astype(ml_dtypes.bfloat16)
    low = (table - high.astype(np.float64)).astype(np.float32).astype(ml_dtypes.bfloat16)
    return high, low


def tables():
    t = np.arange(T)
    angle = 2 * np.pi * (t[:, None] * t[None, :] % T) / T
    high, low = split_table(np.concatenate([np.cos(angle), np.sin(angle)], axis=1))

    def parts(steps, period):
        angles = 2 * np.pi * (steps % period) / period
        return np.stack([np.cos(angles), -np.sin(angles)], axis=-3).astype(np.float32)

    freqs = np.array([item_freqs(i) for i in range(A)])
    places = np.arange(D * T).reshape(D, 1, T)
    slow = parts(freqs[:, None, :, None] * places, FULL).reshape(A, D, 2, ROWS, LANES)
    fast = parts(np.arange(D)[:, None, None] * t * np.ones((1, 2, 1), int), D * T)
    return slow, fast.reshape(D, 2, ROWS, LANES), high, low


VMEM = pl.BlockSpec(memory_space=pltpu.VMEM)
SMEM = pl.BlockSpec(memory_space=pltpu.SMEM)
HBM = pl.BlockSpec(memory_space=pltpu.HBM)


def call(kernel, shape, in_specs, dtype=jnp.float32, scratch=()):
    return pl.pallas_call(
        kernel,
        out_shape=jax.ShapeDtypeStruct(shape, dtype),
        in_specs=in_specs,
        out_specs=VMEM,
        scratch_shapes=list(scratch),
        compiler_params=pltpu.CompilerParams(vmem_limit_bytes=VMEM_LIMIT),
    )


def run_pack(k_proj, v_proj, spectrum):
    return call(
        pack_kernel,
        (N_FAR * SEND_A, LANES),
        [HBM] * 3,
        scratch=[
            pltpu.VMEM(k_proj.shape, k_proj.dtype),
            pltpu.VMEM(v_proj.shape, v_proj.dtype),
            pltpu.VMEM(spectrum.shape, spectrum.dtype),
            pltpu.SemaphoreType.DMA((3,)),
        ],
    )(k_proj, v_proj, spectrum)


def run_coarse(value):
    return call(coarse_kernel, (N_NEAR * SEND_B, LANES), [VMEM])(value)


def run_filter(item, value):
    return call(
        filter_kernel,
        (N_NEAR * SEND_C, LANES),
        [SMEM] + [VMEM] * 5,
        scratch=[pltpu.VMEM((D * ROWS, LANES), jnp.float32)] * 2
        + [pltpu.VMEM((4 * D, T), jnp.bfloat16)] * 2,
    )(item, value, *tables())


def run_uncoarse(value):
    return call(uncoarse_kernel, (N_FAR * ROWS, LANES), [VMEM])(value)


def run_gate(value, q_proj, k_proj, v_proj, skip_gain):
    return call(
        gate_kernel,
        q_proj.shape,
        [VMEM] * 4 + [HBM],
        dtype=jnp.bfloat16,
        scratch=[pltpu.VMEM((1, q_proj.shape[0]), jnp.float32), pltpu.SemaphoreType.DMA],
    )(value, q_proj, k_proj, v_proj, skip_gain.reshape(1, -1))


def exchange(value, axes, count):
    blocks = value.reshape(count, -1, LANES)
    return lax.all_to_all(blocks, axes, 0, 0, tiled=True).reshape(-1, LANES)


def local(q_proj, k_proj, v_proj, skip_gain, spectrum):
    value = run_pack(k_proj, v_proj, spectrum.reshape(4, *k_proj.shape))
    value = exchange(value, FAR, N_FAR)
    value = run_coarse(value)
    value = exchange(value, NEAR, N_NEAR)
    item = (lax.axis_index(NEAR) // 2).astype(jnp.int32).reshape(1)
    value = run_filter(item, value)
    value = exchange(value, NEAR, N_NEAR)
    value = run_uncoarse(value)
    value = exchange(value, FAR, N_FAR)
    return run_gate(value, q_proj, k_proj, v_proj, skip_gain)


def solution(mesh):
    fine = Mesh(mesh.devices.reshape(SIZES), AXES)
    placed = (P(None, AXES), P(None, AXES), P(None, AXES), P(), P(None, None, None, AXES))
    return jax.shard_map(
        local, mesh=fine, in_specs=placed, out_specs=P(None, AXES), check_vma=False
    )
```

time: 104 us -> 99.8 us (0.960)
  blocking collectives: 62.7 us -> 68.9 us
  starting transfers between devices: 12.3 us -> 6.4 us
  waiting for transfers between devices: 19 us -> 13.7 us
  local copies, waits for them, and re-layouts: 3.4 us -> 5.07 us
    all_to_all x3, blocking collectives: 62.7 us -> 68.9 us  [exchange(): return lax.all_to_all(blocks, axes, 0, 0, tiled=True).reshape(-1, LANES)]
    all_to_all x1, starting transfers between devices: 12.3 us -> 6.4 us  [exchange(): return lax.all_to_all(blocks, axes, 0, 0, tiled=True).reshape(-1, LANES)]
    all_to_all x1, waiting for transfers between devices: 19 us -> 13.7 us  [exchange(): return lax.all_to_all(blocks, axes, 0, 0, tiled=True).reshape(-1, LANES)]
    unnamed x24 -> x22, local copies, waits for them, and re-layouts: 3.4 us -> 5.07 us
where the time goes in v1:
time: 99.8 us; the launch traced here: 99.4 us
  blocking collectives  68.9 us (69%)
  waiting for transfers between devices  13.7 us (14%)
  starting transfers between devices  6.4 us (6%)
  Pallas kernels  5.27 us (5%)
  local copies, waits for them, and re-layouts  5.07 us (5%)
    all_to_all x3, blocking collectives, exchange(): return lax.all_to_all(blocks, axes, 0, 0, tiled=True).reshape(-1, LANES)  68.9 us
    all_to_all x1, waiting for transfers between devices, exchange(): return lax.all_to_all(blocks, axes, 0, 0, tiled=True).reshape(-1, LANES)  13.7 us
    all_to_all x1, starting transfers between devices, exchange(): return lax.all_to_all(blocks, axes, 0, 0, tiled=True).reshape(-1, LANES)  6.4 us
    unnamed x22, local copies, waits for them, and re-layouts  5.07 us
    pallas_call x1, Pallas kernels, run_filter(): call(filter_kernel, (N_NEAR * SEND_C, LANES), [SMEM] + [VMEM] * 5, scratc...  3.12 us
  transfers between devices with their start and end apart: 1, of which 1 were waited for; matrix products, arithmetic and copies ran while one was open for 0% of the time, Pallas kernels for 0%

profile of v1, /device:TPU:1, one launch (start us, length us, event | category | flops | bytes accessed | tf_op | source)
XLA Modules:
  0.0 99.4 jit_solution(12597379175255778107)
XLA Ops:
  0.0 0.0 copy-start.1
  0.0 0.0 copy-start.4
  0.0 1.2 %copy-done.4 = f32[2,2,64,512]{3,2,1,0:T(8,128)S(1)} copy-done((f32[2,2,64,512]{3,2,1,0:T(8,128)S(1)}, f32[2,2,64,512]{3,2,1,0:T(8,128)}, u32[]{:S(2)}) %copy-start.4) | copy-done | bytes 524312
  1.2 0.8 copy-done.5
  2.0 0.8 copy-done.7
  2.9 0.3 shard_map.91
  3.2 40.2 %all_to_all.20 = f32[32,40,128]{2,1,0:T(8,128)S(1)} all-to-all(f32[32,40,128]{2,1,0:T(8,128)S(1)} %bitcast.13), channel_id=1, replica_groups=mesh['xl'=2,'yh'=4,'yl'=2,'core'=2,'xh'=2,'zh'=4,'zl'=2] {'xl','yh','zh'}, dimensions={0} | all-to-all | bytes 1310720 | tf_op jit(solution)/shard_map/all_to_all | solution.py:429
  43.4 1.0 shard_map.92
  44.4 6.4 %all-to-all-start.1 = ((f32[16,96,128]{2,1,0:T(8,128)}), f32[16,96,128]{2,1,0:T(8,128)S(1)}, u32[]{:S(2)}, u32[]{:S(2)}) async-start(f32[16,96,128]{2,1,0:T(8,128)} %bitcast.4), calls=%async_computation.1 | async-start | bytes 1572864 | tf_op jit(solution)/shard_map/all_to_all | solution.py:429
  50.8 13.7 %all-to-all-done.1 = f32[16,96,128]{2,1,0:T(8,128)S(1)} async-done(((f32[16,96,128]{2,1,0:T(8,128)}), f32[16,96,128]{2,1,0:T(8,128)S(1)}, u32[]{:S(2)}, u32[]{:S(2)}) %all-to-all-start.1) | async-done | bytes 786464 | tf_op jit(solution)/shard_map/all_to_all | solution.py:429
  64.5 0.0 copy-done.1
  64.5 0.0 copy-done.2
  64.5 0.0 copy-done.3
  64.5 0.0 copy-start
  64.5 2.2 %copy-done = f32[8,64,2,8,128]{4,3,2,1,0:T(8,128)S(1)} copy-done((f32[8,64,2,8,128]{4,3,2,1,0:T(8,128)S(1)}, f32[8,64,2,8,128]{4,3,2,1,0:T(8,128)}, u32[]{:S(2)}) %copy-start) | copy-done | bytes 4194328
  66.7 3.1 %shard_map.93 = f32[512,128]{1,0:T(8,128)S(1)} custom-call(s32[1]{0:T(128)} %bitcast.i_ref, f32[1536,128]{1,0:T(8,128)S(1)} %bitcast.11, f32[8,64,2,8,128]{4,3,2,1,0:T(8,128)S(1)} %copy-done, f32[64,2,8,128]{3,2,1,0:T(8,128)S(1)} %copy-done.3, bf16[512,1024]{1,0:T(8,128)(2,1)S(1)} %copy-done.2, bf16[512,1024]{1,0:T(8,128)(2,1)S(1)} %copy-done.1), custom_call_target="tpu_custom_call" | custom-call | tf_op jit(solution)/shard_map/pallas_call | solution.py:404
  69.8 11.4 %all_to_all.21 = f32[16,32,128]{2,1,0:T(8,128)S(1)} all-to-all(f32[16,32,128]{2,1,0:T(8,128)S(1)} %bitcast.14), channel_id=1, replica_groups=mesh['xl'=2,'yh'=4,'yl'=2,'core'=2,'xh'=2,'zh'=4,'zl'=2] {'yl','core','x..., dimensions={0} | all-to-all | bytes 524288 | tf_op jit(solution)/shard_map/all_to_all | solution.py:429
  81.2 0.1 shard_map.94
  81.3 17.3 %all_to_all.22 = f32[32,8,128]{2,1,0:T(8,128)S(1)} all-to-all(f32[32,8,128]{2,1,0:T(8,128)S(1)} %bitcast.16), channel_id=1, replica_groups=mesh['xl'=2,'yh'=4,'yl'=2,'core'=2,'xh'=2,'zh'=4,'zl'=2] {'xl','yh','zh'}, dimensions={0} | all-to-all | bytes 262144 | tf_op jit(solution)/shard_map/all_to_all | solution.py:429
  98.6 0.0 copy-done.6
  98.6 0.0 copy-done.8
  98.6 0.0 copy-done.9
  98.6 0.0 copy-done.10
  98.6 0.8 shard_map.95
  (8 shorter events, 0.0 us)
Async XLA Ops:
  0.0 64.5 %copy-start.1 = (bf16[512,1024]{1,0:T(8,128)(2,1)S(1)}, bf16[512,1024]{1,0:T(8,128)(2,1)}, u32[]{:S(2)}) copy-start(bf16[512,1024]{1,0:T(8,128)(2,1)} %constant.46.clone.low_ref) | copy-start | bytes 3145732
  0.0 64.5 %copy-start.2 = (bf16[512,1024]{1,0:T(8,128)(2,1)S(1)}, bf16[512,1024]{1,0:T(8,128)(2,1)}, u32[]{:S(2)}) copy-start(bf16[512,1024]{1,0:T(8,128)(2,1)} %constant.45.clone.high_ref) | copy-start | bytes 3145732
  0.0 64.5 %copy-start.3 = (f32[64,2,8,128]{3,2,1,0:T(8,128)S(1)}, f32[64,2,8,128]{3,2,1,0:T(8,128)}, u32[]{:S(2)}) copy-start(f32[64,2,8,128]{3,2,1,0:T(8,128)} %constant.44.clone.fast_ref) | copy-start | bytes 1572868
  0.0 1.2 %copy-start.4 = (f32[2,2,64,512]{3,2,1,0:T(8,128)S(1)}, f32[2,2,64,512]{3,2,1,0:T(8,128)}, u32[]{:S(2)}) copy-start(f32[2,2,64,512]{3,2,1,0:T(8,128)} %param.13) | copy-start | bytes 1572868
  1.2 0.8 copy-start.5
  2.0 0.8 copy-start.7
  44.4 20.1 %all-to-all-start.1 = ((f32[16,96,128]{2,1,0:T(8,128)}), f32[16,96,128]{2,1,0:T(8,128)S(1)}, u32[]{:S(2)}, u32[]{:S(2)}) async-start(f32[16,96,128]{2,1,0:T(8,128)} %bitcast.4), calls=%async_computation.1 | async-start | bytes 1572864 | tf_op jit(solution)/shard_map/all_to_all | solution.py:429
  64.5 2.2 %copy-start = (f32[8,64,2,8,128]{4,3,2,1,0:T(8,128)S(1)}, f32[8,64,2,8,128]{4,3,2,1,0:T(8,128)}, u32[]{:S(2)}) copy-start(f32[8,64,2,8,128]{4,3,2,1,0:T(8,128)} %constant.43.clone.slow_ref) | copy-start | bytes 12582916
  66.7 31.9 %copy-start.6 = (bf16[64,512]{1,0:T(8,128)(2,1)S(1)}, bf16[64,512]{1,0:T(8,128)(2,1)}, u32[]{:S(2)}) copy-start(bf16[64,512]{1,0:T(8,128)(2,1)} %k_ref.1) | copy-start | bytes 196612
  66.7 31.9 %copy-start.8 = (bf16[64,512]{1,0:T(8,128)(2,1)S(1)}, bf16[64,512]{1,0:T(8,128)(2,1)}, u32[]{:S(2)}) copy-start(bf16[64,512]{1,0:T(8,128)(2,1)} %v_ref.1) | copy-start | bytes 196612
  66.7 31.9 %copy-start.9 = (bf16[64,512]{1,0:T(8,128)(2,1)S(1)}, bf16[64,512]{1,0:T(8,128)(2,1)}, u32[]{:S(2)}) copy-start(bf16[64,512]{1,0:T(8,128)(2,1)} %q_ref.1) | copy-start | bytes 196612
  66.7 31.9 %copy-start.10 = (f32[64]{0:T(128)S(1)}, f32[64]{0:T(128)}, u32[]{:S(2)}) copy-start(f32[64]{0:T(128)} %param.12) | copy-start | bytes 772

commit v2 on v1

--- a/solution.py
+++ b/solution.py
@@ -24,6 +24,7 @@
 ROWS = 2 * CHUNKS
 FULL = 2 * A * D * T
 VMEM_LIMIT = 24 * 1024 * 1024
+PACK_LIMIT = 63 * 1024 * 1024
 
 
 def item_freqs(i):
@@ -212,15 +213,16 @@
     return high, (value - high.astype(jnp.float32)).astype(jnp.bfloat16)
 
 
-def dense(high_ref, low_ref, table_high, table_low):
-    def dot(a, b):
-        return jnp.dot(a[...], b[...], preferred_element_type=jnp.float32)
-
-    return dot(high_ref, table_high) + (dot(low_ref, table_high) + dot(high_ref, table_low))
+def dense(high_ref, low_ref, table_ref):
+    def dot(ref, first):
+        table = table_ref[first : first + T, :]
+        return jnp.dot(ref[...], table, preferred_element_type=jnp.float32)
+
+    return dot(high_ref, 0) + (dot(low_ref, 0) + dot(high_ref, T))
 
 
 def filter_kernel(
-    i_ref, in_ref, slow_ref, fast_ref, high_ref, low_ref, out_ref, re_ref, im_ref, xh_ref, xl_ref
+    i_ref, in_ref, turn_ref, table_ref, out_ref, re_ref, im_ref, xh_ref, xl_ref
 ):
     item = i_ref[0]
     packed = item == 0
@@ -234,12 +236,12 @@
             value = in_ref[pl.ds(w * SEND_B + zh * ROWS, ROWS), :]
             other = swap_halves(value)
             pair = (jnp.where(keep, value, other), jnp.where(upper, other, value) * signs)
-            values[d] = times(pair, (slow_ref[item, d, 0], slow_ref[item, d, 1]))
+            values[d] = times(pair, (turn_ref[d, 0], turn_ref[d, 1]))
     for kd, value in enumerate(complex_transform(values, -1)):
         w, zh = freq_place(kd)
         at = (zh * N_NEAR + w) * ROWS
         re_ref[pl.ds(at, ROWS), :], im_ref[pl.ds(at, ROWS), :] = times(
-            value, (fast_ref[kd, 0], fast_ref[kd, 1])
+            value, (turn_ref[D + kd, 0], turn_ref[D + kd, 1])
         )
     half_rows = 2 * D
     blocks = []
@@ -261,7 +263,7 @@
                 high, low = split(ref[pl.ds(start + chunk, N_NEAR, stride=ROWS), :])
                 xh_ref[rows, cols] = high
                 xl_ref[rows, cols] = low
-    mixed = dense(xh_ref, xl_ref, high_ref, low_ref)
+    mixed = dense(xh_ref, xl_ref, table_ref)
     for top, bottom, _, start in blocks:
         for chunk in range(CHUNKS):
             cols = slice(chunk * LANES, (chunk + 1) * LANES)
@@ -278,7 +280,7 @@
                 high, low = split(part)
                 xh_ref[rows, cols] = high
                 xl_ref[rows, cols] = low
-    mixed = dense(xh_ref, xl_ref, high_ref, low_ref)
+    mixed = dense(xh_ref, xl_ref, table_ref)
     for top, bottom, start, _ in blocks:
         for chunk in range(CHUNKS):
             cols = slice(chunk * LANES, (chunk + 1) * LANES)
@@ -291,13 +293,13 @@
         w, zh = freq_place(kd)
         at = (zh * N_NEAR + w) * ROWS
         value = (re_ref[pl.ds(at, ROWS), :], im_ref[pl.ds(at, ROWS), :])
-        values.append(times_conj(value, (fast_ref[kd, 0], fast_ref[kd, 1])))
+        values.append(times_conj(value, (turn_ref[D + kd, 0], turn_ref[D + kd, 1])))
     values = complex_transform(values, 1)
     scale = jnp.where(packed, 1.0 / FULL, 0.5 / FULL)
     for w in range(N_NEAR):
         for zh in range(ZH):
             d = digit(w, zh)
-            re, im = times_conj(values[d], (slow_ref[item, d, 0], slow_ref[item, d, 1]))
+            re, im = times_conj(values[d], (turn_ref[d, 0], turn_ref[d, 1]))
             summed = jnp.where(upper, re + swap_halves(re), swap_halves(im) - im)
             out_ref[pl.ds(w * SEND_C + zh * ROWS, ROWS), :] = (
                 jnp.where(packed, re, summed) * scale
@@ -363,7 +365,8 @@
     places = np.arange(D * T).reshape(D, 1, T)
     slow = parts(freqs[:, None, :, None] * places, FULL).reshape(A, D, 2, ROWS, LANES)
     fast = parts(np.arange(D)[:, None, None] * t * np.ones((1, 2, 1), int), D * T)
-    return slow, fast.reshape(D, 2, ROWS, LANES), high, low
+    fast = np.broadcast_to(fast.reshape(1, D, 2, ROWS, LANES), slow.shape)
+    return np.concatenate([slow, fast], axis=1), high, low
 
 
 VMEM = pl.BlockSpec(memory_space=pltpu.VMEM)
@@ -371,14 +374,14 @@
 HBM = pl.BlockSpec(memory_space=pltpu.HBM)
 
 
-def call(kernel, shape, in_specs, dtype=jnp.float32, scratch=()):
+def call(kernel, shape, in_specs, dtype=jnp.float32, scratch=(), limit=VMEM_LIMIT):
     return pl.pallas_call(
         kernel,
         out_shape=jax.ShapeDtypeStruct(shape, dtype),
         in_specs=in_specs,
         out_specs=VMEM,
         scratch_shapes=list(scratch),
-        compiler_params=pltpu.CompilerParams(vmem_limit_bytes=VMEM_LIMIT),
+        compiler_params=pltpu.CompilerParams(vmem_limit_bytes=limit),
     )
 
 
@@ -393,6 +396,7 @@
             pltpu.VMEM(spectrum.shape, spectrum.dtype),
             pltpu.SemaphoreType.DMA((3,)),
         ],
+        limit=PACK_LIMIT,
     )(k_proj, v_proj, spectrum)
 
 
@@ -401,13 +405,18 @@
 
 
 def run_filter(item, value):
+    turns, high, low = tables()
+    turns = lax.dynamic_index_in_dim(turns, item[0], keepdims=False)
+    dense_table = lax.dynamic_index_in_dim(
+        np.stack([np.concatenate([high, low])] * 2), item[0] % 2, keepdims=False
+    )
     return call(
         filter_kernel,
         (N_NEAR * SEND_C, LANES),
-        [SMEM] + [VMEM] * 5,
+        [SMEM] + [VMEM] * 3,
         scratch=[pltpu.VMEM((D * ROWS, LANES), jnp.float32)] * 2
         + [pltpu.VMEM((4 * D, T), jnp.bfloat16)] * 2,
-    )(item, value, *tables())
+    )(item, value, turns, dense_table)
 
 
 def run_uncoarse(value):

time: 99.8 us -> 98.1 us (0.983)
  waiting for transfers between devices: 13.7 us -> 10.6 us
  Pallas kernels: 5.27 us -> 8.25 us
  local copies, waits for them, and re-layouts: 5.07 us -> 3.14 us
    unnamed x22 -> x8, local copies, waits for them, and re-layouts: 5.07 us -> 0.03 us
    squeeze x0 -> x2, local copies, waits for them, and re-layouts: none -> 3.12 us  [the longest x1 1.82 us: run_filter(): lax.dynamic_index_in_dim(np.stack([np.concatenate([high, low])] * 2), ite...]
    all_to_all x1, waiting for transfers between devices: 13.7 us -> 10.6 us  [exchange(): return lax.all_to_all(blocks, axes, 0, 0, tiled=True).reshape(-1, LANES)]
    pallas_call x1, Pallas kernels: 0.31 us -> 2.08 us  [run_pack(): call(pack_kernel, (N_FAR * SEND_A, LANES), [HBM] * 3, scratch=[pltpu.VMEM...]
    pallas_call x1, Pallas kernels: 3.12 us -> 4.34 us  [run_filter(): call(filter_kernel, (N_NEAR * SEND_C, LANES), [SMEM] + [VMEM] * 3, scratc...]
  transfers between devices with their start and end apart: 1 -> 1, of which waited for: 1 -> 1; matrix products, arithmetic and copies ran while one was open for 0% -> 3% of each run, Pallas kernels for 0% -> 0%
where the time goes in v2:
time: 98.1 us; the launch traced here: 97.6 us
  blocking collectives  69.1 us (70%)
  waiting for transfers between devices  10.6 us (11%)
  Pallas kernels  8.25 us (8%)
  starting transfers between devices  6.39 us (7%)
  local copies, waits for them, and re-layouts  3.14 us (3%)
    all_to_all x3, blocking collectives, exchange(): return lax.all_to_all(blocks, axes, 0, 0, tiled=True).reshape(-1, LANES)  69.1 us
    all_to_all x1, waiting for transfers between devices, exchange(): return lax.all_to_all(blocks, axes, 0, 0, tiled=True).reshape(-1, LANES)  10.6 us
    all_to_all x1, starting transfers between devices, exchange(): return lax.all_to_all(blocks, axes, 0, 0, tiled=True).reshape(-1, LANES)  6.39 us
    pallas_call x1, Pallas kernels, run_filter(): call(filter_kernel, (N_NEAR * SEND_C, LANES), [SMEM] + [VMEM] * 3, scratc...  4.34 us
    pallas_call x1, Pallas kernels, run_pack(): call(pack_kernel, (N_FAR * SEND_A, LANES), [HBM] * 3, scratch=[pltpu.VMEM...  2.08 us
  transfers between devices with their start and end apart: 1, of which 1 were waited for; matrix products, arithmetic and copies ran while one was open for 3% of the time, Pallas kernels for 0%

profile of v2, /device:TPU:1, one launch (start us, length us, event | category | flops | bytes accessed | tf_op | source)
XLA Modules:
  0.0 97.6 jit_solution(9901782959745692709)
XLA Ops:
  0.0 2.1 %shard_map.73 = f32[1280,128]{1,0:T(8,128)} custom-call(bf16[64,512]{1,0:T(8,128)(2,1)} %k_ref.1, bf16[64,512]{1,0:T(8,128)(2,1)} %v_ref.1, f32[4,64,512]{2,1,0:T(8,128)} %bitcast.22), custom_call_target="tpu_custom_call" | custom-call | tf_op jit(solution)/shard_map/pallas_call | solution.py:389
  2.1 40.4 %all_to_all.20 = f32[32,40,128]{2,1,0:T(8,128)S(1)} all-to-all(f32[32,40,128]{2,1,0:T(8,128)} %bitcast.21), channel_id=1, replica_groups=mesh['xl'=2,'yh'=4,'yl'=2,'core'=2,'xh'=2,'zh'=4,'zl'=2] {'xl','yh','zh'}, dimensions={0} | all-to-all | bytes 1310720 | tf_op jit(solution)/shard_map/all_to_all | solution.py:438
  42.5 1.0 %shard_map.74 = f32[1536,128]{1,0:T(8,128)} custom-call(f32[1280,128]{1,0:T(8,128)S(1)} %bitcast.15), custom_call_target="tpu_custom_call" | custom-call | tf_op jit(solution)/shard_map/pallas_call | solution.py:404
  43.5 6.4 %all-to-all-start.1 = ((f32[16,96,128]{2,1,0:T(8,128)}), f32[16,96,128]{2,1,0:T(8,128)}, u32[]{:S(2)}, u32[]{:S(2)}) async-start(f32[16,96,128]{2,1,0:T(8,128)} %bitcast.4), calls=%async_computation.1 | async-start | bytes 1572864 | tf_op jit(solution)/shard_map/all_to_all | solution.py:438
  49.9 1.3 %dynamic-slice_bitcast_fusion.1.turn_ref = f32[128,2,8,128]{3,2,1,0:T(8,128)S(1)} fusion(f32[8,128,2,8,128]{4,3,2,1,0:T(8,128)} %constant.56.clone, s32[]{:T(128)S(6)} %select_n.20), kind=kLoop, calls=%fused_computation.1 | loop fusion | bytes 2097156 | tf_op jit(solution)/shard_map/jit(dynamic_index_in_dim)/squeeze | solution.py:409
  51.2 0.0 copy-start
  51.2 0.0 copy-start.1
  51.2 0.0 copy-start.2
  51.2 0.0 copy-start.3
  51.2 1.8 %dynamic-slice_bitcast_fusion.table_ref = bf16[1024,1024]{1,0:T(8,128)(2,1)S(1)} fusion(bf16[2,1024,1024]{2,1,0:T(8,128)(2,1)} %constant.57.clone, s32[]{:T(128)S(6)} %select_n.22), kind=kLoop, calls=%fused_computation | loop fusion | bytes 4194308 | tf_op jit(solution)/shard_map/jit(dynamic_index_in_dim)/squeeze | solution.py:410
  53.1 10.6 %all-to-all-done.1 = f32[16,96,128]{2,1,0:T(8,128)} async-done(((f32[16,96,128]{2,1,0:T(8,128)}), f32[16,96,128]{2,1,0:T(8,128)}, u32[]{:S(2)}, u32[]{:S(2)}) %all-to-all-start.1) | async-done | bytes 786464 | tf_op jit(solution)/shard_map/all_to_all | solution.py:438
  63.7 4.3 %shard_map.75 = f32[512,128]{1,0:T(8,128)S(1)} custom-call(s32[1]{0:T(128)} %bitcast.i_ref, f32[1536,128]{1,0:T(8,128)} %bitcast.5.in_ref, f32[128,2,8,128]{3,2,1,0:T(8,128)S(1)} %dynamic-slice_bitcast_fusion.1.turn_ref, bf16[1024,1024]{1,0:T(8,128)(2,1)S(1)} %dynamic-slice_bitcast_fusion.table_ref), custom_call_target="tpu_custom_call" | custom-call | tf_op jit(solution)/shard_map/pallas_call | solution.py:413
  68.0 11.4 %all_to_all.21 = f32[16,32,128]{2,1,0:T(8,128)S(1)} all-to-all(f32[16,32,128]{2,1,0:T(8,128)S(1)} %bitcast.16), channel_id=1, replica_groups=mesh['xl'=2,'yh'=4,'yl'=2,'core'=2,'xh'=2,'zh'=4,'zl'=2] {'yl','core','x..., dimensions={0} | all-to-all | bytes 524288 | tf_op jit(solution)/shard_map/all_to_all | solution.py:438
  79.4 0.1 shard_map.76
  79.5 17.3 %all_to_all.22 = f32[32,8,128]{2,1,0:T(8,128)S(1)} all-to-all(f32[32,8,128]{2,1,0:T(8,128)S(1)} %bitcast.18), channel_id=1, replica_groups=mesh['xl'=2,'yh'=4,'yl'=2,'core'=2,'xh'=2,'zh'=4,'zl'=2] {'xl','yh','zh'}, dimensions={0} | all-to-all | bytes 262144 | tf_op jit(solution)/shard_map/all_to_all | solution.py:438
  96.8 0.0 copy-done
  96.8 0.0 copy-done.1
  96.8 0.0 copy-done.2
  96.8 0.0 copy-done.3
  96.8 0.8 shard_map.77
Async XLA Ops:
  43.5 20.2 %all-to-all-start.1 = ((f32[16,96,128]{2,1,0:T(8,128)}), f32[16,96,128]{2,1,0:T(8,128)}, u32[]{:S(2)}, u32[]{:S(2)}) async-start(f32[16,96,128]{2,1,0:T(8,128)} %bitcast.4), calls=%async_computation.1 | async-start | bytes 1572864 | tf_op jit(solution)/shard_map/all_to_all | solution.py:438
  51.2 45.6 %copy-start = (bf16[64,512]{1,0:T(8,128)(2,1)S(1)}, bf16[64,512]{1,0:T(8,128)(2,1)}, u32[]{:S(2)}) copy-start(bf16[64,512]{1,0:T(8,128)(2,1)} %k_ref.1) | copy-start | bytes 196612
  51.2 45.6 %copy-start.1 = (bf16[64,512]{1,0:T(8,128)(2,1)S(1)}, bf16[64,512]{1,0:T(8,128)(2,1)}, u32[]{:S(2)}) copy-start(bf16[64,512]{1,0:T(8,128)(2,1)} %v_ref.1) | copy-start | bytes 196612
  51.2 45.6 %copy-start.2 = (bf16[64,512]{1,0:T(8,128)(2,1)S(1)}, bf16[64,512]{1,0:T(8,128)(2,1)}, u32[]{:S(2)}) copy-start(bf16[64,512]{1,0:T(8,128)(2,1)} %q_ref.1) | copy-start | bytes 196612
  51.2 45.6 %copy-start.3 = (f32[64]{0:T(128)S(1)}, f32[64]{0:T(128)}, u32[]{:S(2)}) copy-start(f32[64]{0:T(128)} %param.10) | copy-start | bytes 772

commit v3 on v2

--- a/solution.py
+++ b/solution.py
@@ -23,8 +23,7 @@
 CHUNKS = T // LANES
 ROWS = 2 * CHUNKS
 FULL = 2 * A * D * T
-VMEM_LIMIT = 24 * 1024 * 1024
-PACK_LIMIT = 63 * 1024 * 1024
+VMEM_LIMIT = 12 * 1024 * 1024
 
 
 def item_freqs(i):
@@ -222,8 +221,13 @@
 
 
 def filter_kernel(
-    i_ref, in_ref, turn_ref, table_ref, out_ref, re_ref, im_ref, xh_ref, xl_ref
+    i_ref, in_ref, slow_ref, fast_hbm, table_hbm, out_ref,
+    re_ref, im_ref, xh_ref, xl_ref, fast_ref, table_ref, sems,
 ):
+    fast_copy = pltpu.make_async_copy(fast_hbm, fast_ref, sems.at[0])
+    table_copy = pltpu.make_async_copy(table_hbm, table_ref, sems.at[1])
+    fast_copy.start()
+    table_copy.start()
     item = i_ref[0]
     packed = item == 0
     upper = upper_rows()
@@ -236,12 +240,13 @@
             value = in_ref[pl.ds(w * SEND_B + zh * ROWS, ROWS), :]
             other = swap_halves(value)
             pair = (jnp.where(keep, value, other), jnp.where(upper, other, value) * signs)
-            values[d] = times(pair, (turn_ref[d, 0], turn_ref[d, 1]))
+            values[d] = times(pair, (slow_ref[d, 0], slow_ref[d, 1]))
+    fast_copy.wait()
     for kd, value in enumerate(complex_transform(values, -1)):
         w, zh = freq_place(kd)
         at = (zh * N_NEAR + w) * ROWS
         re_ref[pl.ds(at, ROWS), :], im_ref[pl.ds(at, ROWS), :] = times(
-            value, (turn_ref[D + kd, 0], turn_ref[D + kd, 1])
+            value, (fast_ref[kd, 0], fast_ref[kd, 1])
         )
     half_rows = 2 * D
     blocks = []
@@ -263,6 +268,7 @@
                 high, low = split(ref[pl.ds(start + chunk, N_NEAR, stride=ROWS), :])
                 xh_ref[rows, cols] = high
                 xl_ref[rows, cols] = low
+    table_copy.wait()
     mixed = dense(xh_ref, xl_ref, table_ref)
     for top, bottom, _, start in blocks:
         for chunk in range(CHUNKS):
@@ -293,13 +299,13 @@
         w, zh = freq_place(kd)
         at = (zh * N_NEAR + w) * ROWS
         value = (re_ref[pl.ds(at, ROWS), :], im_ref[pl.ds(at, ROWS), :])
-        values.append(times_conj(value, (turn_ref[D + kd, 0], turn_ref[D + kd, 1])))
+        values.append(times_conj(value, (fast_ref[kd, 0], fast_ref[kd, 1])))
     values = complex_transform(values, 1)
     scale = jnp.where(packed, 1.0 / FULL, 0.5 / FULL)
     for w in range(N_NEAR):
         for zh in range(ZH):
             d = digit(w, zh)
-            re, im = times_conj(values[d], (turn_ref[d, 0], turn_ref[d, 1]))
+            re, im = times_conj(values[d], (slow_ref[d, 0], slow_ref[d, 1]))
             summed = jnp.where(upper, re + swap_halves(re), swap_halves(im) - im)
             out_ref[pl.ds(w * SEND_C + zh * ROWS, ROWS), :] = (
                 jnp.where(packed, re, summed) * scale
@@ -365,13 +371,16 @@
     places = np.arange(D * T).reshape(D, 1, T)
     slow = parts(freqs[:, None, :, None] * places, FULL).reshape(A, D, 2, ROWS, LANES)
     fast = parts(np.arange(D)[:, None, None] * t * np.ones((1, 2, 1), int), D * T)
-    fast = np.broadcast_to(fast.reshape(1, D, 2, ROWS, LANES), slow.shape)
-    return np.concatenate([slow, fast], axis=1), high, low
+    return slow, fast.reshape(D, 2, ROWS, LANES), np.concatenate([high, low])
 
 
 VMEM = pl.BlockSpec(memory_space=pltpu.VMEM)
 SMEM = pl.BlockSpec(memory_space=pltpu.SMEM)
 HBM = pl.BlockSpec(memory_space=pltpu.HBM)
+
+
+def in_hbm(x):
+    return pltpu.with_memory_space_constraint(jnp.asarray(x), pltpu.HBM)
 
 
 def call(kernel, shape, in_specs, dtype=jnp.float32, scratch=(), limit=VMEM_LIMIT):
@@ -396,8 +405,7 @@
             pltpu.VMEM(spectrum.shape, spectrum.dtype),
             pltpu.SemaphoreType.DMA((3,)),
         ],
-        limit=PACK_LIMIT,
-    )(k_proj, v_proj, spectrum)
+    )(*(in_hbm(x) for x in (k_proj, v_proj, spectrum)))
 
 
 def run_coarse(value):
@@ -405,18 +413,20 @@
 
 
 def run_filter(item, value):
-    turns, high, low = tables()
-    turns = lax.dynamic_index_in_dim(turns, item[0], keepdims=False)
-    dense_table = lax.dynamic_index_in_dim(
-        np.stack([np.concatenate([high, low])] * 2), item[0] % 2, keepdims=False
-    )
+    slow, fast, table = tables()
+    slow = lax.dynamic_index_in_dim(slow, item[0], keepdims=False)
     return call(
         filter_kernel,
         (N_NEAR * SEND_C, LANES),
-        [SMEM] + [VMEM] * 3,
+        [SMEM] + [VMEM] * 2 + [HBM] * 2,
         scratch=[pltpu.VMEM((D * ROWS, LANES), jnp.float32)] * 2
-        + [pltpu.VMEM((4 * D, T), jnp.bfloat16)] * 2,
-    )(item, value, turns, dense_table)
+        + [pltpu.VMEM((4 * D, T), jnp.bfloat16)] * 2
+        + [
+            pltpu.VMEM(fast.shape, jnp.float32),
+            pltpu.VMEM(table.shape, jnp.bfloat16),
+            pltpu.SemaphoreType.DMA((2,)),
+        ],
+    )(item, value, slow, *(in_hbm(x) for x in (fast, table)))
 
 
 def run_uncoarse(value):

time: 98.1 us -> 97.2 us (level)
  local copies, waits for them, and re-layouts: 3.14 us -> 1.09 us
  waiting for transfers between devices: 10.6 us -> 12.6 us
    squeeze x2 -> x1, local copies, waits for them, and re-layouts: 3.12 us -> 1.08 us  [run_filter(): slow = lax.dynamic_index_in_dim(slow, item[0], keepdims=False)]
    all_to_all x1, waiting for transfers between devices: 10.6 us -> 12.6 us  [exchange(): return lax.all_to_all(blocks, axes, 0, 0, tiled=True).reshape(-1, LANES)]
  transfers between devices with their start and end apart: 1 -> 1, of which waited for: 1 -> 1; matrix products, arithmetic and copies ran while one was open for 3% -> 1% of each run, Pallas kernels for 0% -> 0%
where the time goes in v3:
time: 97.2 us; the launch traced here: 96.8 us
  blocking collectives  68.9 us (71%)
  waiting for transfers between devices  12.6 us (13%)
  Pallas kernels  7.57 us (8%)
  starting transfers between devices  6.54 us (7%)
  local copies, waits for them, and re-layouts  1.09 us (1%)
    all_to_all x3, blocking collectives, exchange(): return lax.all_to_all(blocks, axes, 0, 0, tiled=True).reshape(-1, LANES)  68.9 us
    all_to_all x1, waiting for transfers between devices, exchange(): return lax.all_to_all(blocks, axes, 0, 0, tiled=True).reshape(-1, LANES)  12.6 us
    all_to_all x1, starting transfers between devices, exchange(): return lax.all_to_all(blocks, axes, 0, 0, tiled=True).reshape(-1, LANES)  6.54 us
    pallas_call x1, Pallas kernels, run_filter(): call(filter_kernel, (N_NEAR * SEND_C, LANES), [SMEM] + [VMEM] * 2 + [HBM]...  4.5 us
  transfers between devices with their start and end apart: 1, of which 1 were waited for; matrix products, arithmetic and copies ran while one was open for 1% of the time, Pallas kernels for 0%

profile of v3, /device:TPU:1, one launch (start us, length us, event | category | flops | bytes accessed | tf_op | source)
XLA Modules:
  0.0 96.8 jit_solution(15779162477934724346)
XLA Ops:
  0.0 1.2 %shard_map.82 = f32[1280,128]{1,0:T(8,128)S(1)} custom-call(bf16[64,512]{1,0:T(8,128)(2,1)} %k_ref.1, bf16[64,512]{1,0:T(8,128)(2,1)} %v_ref.1, f32[4,64,512]{2,1,0:T(8,128)} %bitcast.21), custom_call_target="tpu_custom_call" | custom-call | tf_op jit(solution)/shard_map/pallas_call | solution.py:398
  1.2 40.2 %all_to_all.20 = f32[32,40,128]{2,1,0:T(8,128)S(1)} all-to-all(f32[32,40,128]{2,1,0:T(8,128)S(1)} %bitcast.15), channel_id=1, replica_groups=mesh['xl'=2,'yh'=4,'yl'=2,'core'=2,'xh'=2,'zh'=4,'zl'=2] {'xl','yh','zh'}, dimensions={0} | all-to-all | bytes 1310720 | tf_op jit(solution)/shard_map/all_to_all | solution.py:448
  41.5 1.0 %shard_map.83 = f32[1536,128]{1,0:T(8,128)} custom-call(f32[1280,128]{1,0:T(8,128)S(1)} %bitcast.14), custom_call_target="tpu_custom_call" | custom-call | tf_op jit(solution)/shard_map/pallas_call | solution.py:412
  42.5 0.0 copy-start
  42.5 0.0 copy-start.1
  42.5 0.0 copy-start.2
  42.5 0.0 copy-start.3
  42.5 6.5 %all-to-all-start.1 = ((f32[16,96,128]{2,1,0:T(8,128)}), f32[16,96,128]{2,1,0:T(8,128)S(1)}, u32[]{:S(2)}, u32[]{:S(2)}) async-start(f32[16,96,128]{2,1,0:T(8,128)} %bitcast.4), calls=%async_computation.1 | async-start | bytes 1572864 | tf_op jit(solution)/shard_map/all_to_all | solution.py:448
  49.0 1.1 %dynamic-slice_bitcast_fusion.slow_ref = f32[64,2,8,128]{3,2,1,0:T(8,128)S(1)} fusion(f32[8,64,2,8,128]{4,3,2,1,0:T(8,128)} %constant.45.clone, s32[]{:T(128)S(6)} %select_n.10), kind=kLoop, calls=%fused_computation | loop fusion | bytes 1048580 | tf_op jit(solution)/shard_map/jit(dynamic_index_in_dim)/squeeze | solution.py:417
  50.1 12.6 %all-to-all-done.1 = f32[16,96,128]{2,1,0:T(8,128)S(1)} async-done(((f32[16,96,128]{2,1,0:T(8,128)}), f32[16,96,128]{2,1,0:T(8,128)S(1)}, u32[]{:S(2)}, u32[]{:S(2)}) %all-to-all-start.1) | async-done | bytes 786464 | tf_op jit(solution)/shard_map/all_to_all | solution.py:448
  62.7 4.5 %shard_map.84 = f32[512,128]{1,0:T(8,128)S(1)} custom-call(s32[1]{0:T(128)} %bitcast.i_ref, f32[1536,128]{1,0:T(8,128)S(1)} %bitcast.13, f32[64,2,8,128]{3,2,1,0:T(8,128)S(1)} %dynamic-slice_bitcast_fusion.slow_ref, f32[64,2,8,128]{3,2,1,0:T(8,128)} %constant.46.clone.fast_hbm, bf16[1024,1024]{1,0:T(8,128)(2,1)} %constant.47.clone.table_hbm), custom_call_target="tpu_custom_call" | custom-call | tf_op jit(solution)/shard_map/pallas_call | solution.py:418
  67.2 11.4 %all_to_all.21 = f32[16,32,128]{2,1,0:T(8,128)S(1)} all-to-all(f32[16,32,128]{2,1,0:T(8,128)S(1)} %bitcast.16), channel_id=1, replica_groups=mesh['xl'=2,'yh'=4,'yl'=2,'core'=2,'xh'=2,'zh'=4,'zl'=2] {'yl','core','x..., dimensions={0} | all-to-all | bytes 524288 | tf_op jit(solution)/shard_map/all_to_all | solution.py:448
  78.6 0.1 shard_map.85
  78.7 17.3 %all_to_all.22 = f32[32,8,128]{2,1,0:T(8,128)S(1)} all-to-all(f32[32,8,128]{2,1,0:T(8,128)S(1)} %bitcast.18), channel_id=1, replica_groups=mesh['xl'=2,'yh'=4,'yl'=2,'core'=2,'xh'=2,'zh'=4,'zl'=2] {'xl','yh','zh'}, dimensions={0} | all-to-all | bytes 262144 | tf_op jit(solution)/shard_map/all_to_all | solution.py:448
  96.0 0.0 copy-done
  96.0 0.0 copy-done.1
  96.0 0.0 copy-done.2
  96.0 0.0 copy-done.3
  96.0 0.8 shard_map.86
Async XLA Ops:
  42.5 53.5 %copy-start = (bf16[64,512]{1,0:T(8,128)(2,1)S(1)}, bf16[64,512]{1,0:T(8,128)(2,1)}, u32[]{:S(2)}) copy-start(bf16[64,512]{1,0:T(8,128)(2,1)} %k_ref.1) | copy-start | bytes 196612
  42.5 53.5 %copy-start.1 = (bf16[64,512]{1,0:T(8,128)(2,1)S(1)}, bf16[64,512]{1,0:T(8,128)(2,1)}, u32[]{:S(2)}) copy-start(bf16[64,512]{1,0:T(8,128)(2,1)} %v_ref.1) | copy-start | bytes 196612
  42.5 53.5 %copy-start.2 = (bf16[64,512]{1,0:T(8,128)(2,1)S(1)}, bf16[64,512]{1,0:T(8,128)(2,1)}, u32[]{:S(2)}) copy-start(bf16[64,512]{1,0:T(8,128)(2,1)} %q_ref.1) | copy-start | bytes 196612
  42.5 53.5 %copy-start.3 = (f32[64]{0:T(128)S(1)}, f32[64]{0:T(128)}, u32[]{:S(2)}) copy-start(f32[64]{0:T(128)} %param.11) | copy-start | bytes 772
  42.5 20.2 %all-to-all-start.1 = ((f32[16,96,128]{2,1,0:T(8,128)}), f32[16,96,128]{2,1,0:T(8,128)S(1)}, u32[]{:S(2)}, u32[]{:S(2)}) async-start(f32[16,96,128]{2,1,0:T(8,128)} %bitcast.4), calls=%async_computation.1 | async-start | bytes 1572864 | tf_op jit(solution)/shard_map/all_to_all | solution.py:448

commit v4 on v1

v4 whole, which is shorter than its diff:
```python
import math

import jax
import jax.numpy as jnp
import ml_dtypes
import numpy as np
from jax import lax
from jax.experimental import pallas as pl
from jax.experimental.pallas import tpu as pltpu
from jax.sharding import Mesh, PartitionSpec as P

AXES = ("xl", "yh", "yl", "core", "xh", "zh", "zl")
SIZES = (2, 4, 2, 2, 2, 4, 2)
FAR = ("xl", "yh", "yl", "zh")
NEAR = ("core", "xh", "zl")
A = 8
B = 8
N_FAR = A * B
N_NEAR = 8
D = B * N_NEAR
T = 512
LANES = 128
CHUNKS = T // LANES
ROWS = 2 * CHUNKS
FULL = 2 * A * D * T
VMEM_LIMIT = 12 * 1024 * 1024


def item_freqs(i):
    return (0, 8) if i == 0 else (i, 16 - i)


def source_of(q):
    xl, y2, y1 = q >> 1 & 1, q >> 2 & 1, q >> 3 & 1
    return q & 1, xl * 4 + y2 * 2 + y1


def digit(w, b):
    core, xh, zl = w >> 2, w >> 1 & 1, w & 1
    yl, zh = b >> 2, b & 3
    return yl * 32 + core * 16 + xh * 8 + zh * 2 + zl


def freq_place(kd):
    y0, core, z0, z1, z2, xh = (kd >> bit & 1 for bit in range(6))
    return core * 4 + xh * 2 + z0, y0 * 4 + z2 * 2 + z1


def add(a, b):
    if a is None:
        return b
    return a if b is None else a + b


def sub(a, b):
    if b is None:
        return a
    return -b if a is None else a - b


def twist(value, steps, period):
    re, im = value
    eighth = 8 * steps % (8 * period)
    if eighth == 0:
        return value
    if eighth == 2 * period:
        return -im, re
    if eighth == 4 * period:
        return -re, -im
    if eighth == 6 * period:
        return im, -re
    c = math.cos(2 * math.pi * steps / period)
    s = math.sin(2 * math.pi * steps / period)
    if abs(abs(c) - abs(s)) < 1e-12:
        r = math.sqrt(0.5)
        cs, ss = math.copysign(1.0, c), math.copysign(1.0, s)
        a = re if cs > 0 else -re
        b = im if cs > 0 else -im
        return (
            ((a - im) if ss > 0 else (a + im)) * r,
            ((b + re) if ss > 0 else (b - re)) * r,
        )
    return re * c - im * s, re * s + im * c


def real_forward(x):
    n = len(x)
    if n == 2:
        return [(add(x[0], x[1]), None), (sub(x[0], x[1]), None)]
    even, odd = real_forward(x[0::2]), real_forward(x[1::2])
    out = [None] * (n // 2 + 1)
    out[0] = (even[0][0] + odd[0][0], None)
    out[n // 2] = (even[0][0] - odd[0][0], None)
    out[n // 4] = (even[n // 4][0], -odd[n // 4][0])
    for k in range(1, n // 4):
        tr, ti = twist(odd[k], -k, n)
        er, ei = even[k]
        out[k] = (er + tr, ei + ti)
        out[n // 2 - k] = (er - tr, ti - ei)
    return out


def real_inverse(x):
    n = 2 * (len(x) - 1)
    if n == 2:
        return [x[0][0] + x[1][0]]
    even, odd = [None] * (n // 4 + 1), [None] * (n // 4 + 1)
    even[0] = (x[0][0] + x[n // 2][0], None)
    odd[0] = (x[0][0] - x[n // 2][0], None)
    even[n // 4] = (2.0 * x[n // 4][0], None)
    odd[n // 4] = (-2.0 * x[n // 4][1], None)
    for k in range(1, n // 4):
        ar, ai = x[k]
        br, bi = x[n // 2 - k]
        even[k] = (ar + br, ai - bi)
        odd[k] = twist((ar - br, ai + bi), k, n)
    out = [None] * (n // 2)
    out[0::2], out[1::2] = real_inverse(even), real_inverse(odd)
    return out


def complex_transform(x, sign):
    n = len(x)
    if n == 1:
        return x
    even, odd = complex_transform(x[0::2], sign), complex_transform(x[1::2], sign)
    low, high = [], []
    for k in range(n // 2):
        tr, ti = twist(odd[k], sign * k, n)
        er, ei = even[k]
        low.append((er + tr, ei + ti))
        high.append((er - tr, ei - ti))
    return low + high


def times(a, b):
    return a[0] * b[0] - a[1] * b[1], a[0] * b[1] + a[1] * b[0]


def times_conj(a, b):
    return a[0] * b[0] + a[1] * b[1], a[1] * b[0] - a[0] * b[1]


SEND_A = 5 * CHUNKS
SEND_B = 3 * B * ROWS
SEND_C = B * ROWS


def pack_kernel(k_hbm, v_hbm, spec_hbm, out_ref, k_ref, v_ref, spec_ref, sems):
    copies = [
        pltpu.make_async_copy(source, target, sems.at[i])
        for i, (source, target) in enumerate(
            ((k_hbm, k_ref), (v_hbm, v_ref), (spec_hbm, spec_ref))
        )
    ]
    for copy in copies:
        copy.start()
    copies[0].wait()
    copies[1].wait()
    product = k_ref[...].astype(jnp.float32) * v_ref[...].astype(jnp.float32)
    for chunk in range(CHUNKS):
        cols = slice(chunk * LANES, (chunk + 1) * LANES)
        out_ref[pl.ds(chunk, N_FAR, stride=SEND_A), :] = product[:, cols]
    copies[2].wait()
    for part in range(4):
        for chunk in range(CHUNKS):
            cols = slice(chunk * LANES, (chunk + 1) * LANES)
            place = (1 + part) * CHUNKS + chunk
            out_ref[pl.ds(place, N_FAR, stride=SEND_A), :] = spec_ref[part, :, cols]


def coarse_kernel(in_ref, out_ref):
    for b in range(B):
        tokens = [in_ref[pl.ds((a * B + b) * SEND_A, CHUNKS), :] for a in range(A)]
        freqs = real_forward(tokens + [None] * A)
        items = [(freqs[0][0], freqs[A][0])] + freqs[1:A]
        for i in range(A):
            for part in range(2):
                target = i * SEND_B + b * ROWS + part * CHUNKS
                out_ref[pl.ds(target, CHUNKS), :] = items[i][part]
                for side, q in enumerate(item_freqs(i)):
                    parity, a = source_of(q)
                    source = (a * B + b) * SEND_A + (1 + 2 * parity + part) * CHUNKS
                    target = i * SEND_B + (B + side * B + b) * ROWS + part * CHUNKS
                    out_ref[pl.ds(target, CHUNKS), :] = in_ref[pl.ds(source, CHUNKS), :]


def upper_rows():
    return lax.broadcasted_iota(jnp.int32, (ROWS, LANES), 0) < CHUNKS


def swap_halves(value):
    return pltpu.roll(value, CHUNKS, 0)


def split(value):
    high = value.astype(jnp.bfloat16)
    return high, (value - high.astype(jnp.float32)).astype(jnp.bfloat16)


def dense(xh_ref, xl_ref, high_ref, low_ref):
    def dot(a, b):
        return jnp.dot(a[...], b[...], preferred_element_type=jnp.float32)

    return dot(xh_ref, high_ref) + (dot(xl_ref, high_ref) + dot(xh_ref, low_ref))


def filter_kernel(
    place_ref, in_ref, gain_hbm, turn_ref, high_ref, low_ref, out_ref,
    re_ref, im_ref, xh_ref, xl_ref, gain_ref, sem,
):
    gain_copy = pltpu.make_async_copy(gain_hbm, gain_ref, sem)
    gain_copy.start()
    channel, item = place_ref[0], place_ref[1]
    packed = item == 0
    upper = upper_rows()
    keep = jnp.logical_or(upper, packed)
    signs = jnp.where(upper, 1.0, -1.0) * jnp.where(packed, 0.0, 1.0)
    steps = turn_ref[D + A + item // 2, item % 2]

    def turned(d):
        return tuple(
            jnp.broadcast_to(steps[:, at : at + 1], (ROWS, LANES)) for at in (d, D + d)
        )

    slow = (turn_ref[D + item, 0], turn_ref[D + item, 1])
    values = [None] * D
    for w in range(N_NEAR):
        for b in range(B):
            d = digit(w, b)
            value = in_ref[pl.ds(w * SEND_B + b * ROWS, ROWS), :]
            other = swap_halves(value)
            pair = (jnp.where(keep, value, other), jnp.where(upper, other, value) * signs)
            values[d] = times(times(pair, slow), turned(d))
    for kd, value in enumerate(complex_transform(values, -1)):
        w, b = freq_place(kd)
        at = (b * N_NEAR + w) * ROWS
        re_ref[pl.ds(at, ROWS), :], im_ref[pl.ds(at, ROWS), :] = times(
            value, (turn_ref[kd, 0], turn_ref[kd, 1])
        )
    gain_copy.wait()
    lane = lax.broadcasted_iota(jnp.int32, gain_ref.shape, 1)
    gain = jnp.sum(jnp.where(lane == channel, gain_ref[...], 0.0))
    half_rows = 2 * D
    step = 2 * N_NEAR
    blocks = []
    for side in range(2):
        for b in range(0, B, 2):
            first = (side * B + b) * N_NEAR
            blocks.append(
                (
                    slice(first, first + step),
                    slice(half_rows + first, half_rows + first + step),
                    b * N_NEAR * ROWS + side * CHUNKS,
                    (B + side * B + b) * ROWS,
                )
            )
    for top, bottom, start, _ in blocks:
        for rows, ref in ((top, re_ref), (bottom, im_ref)):
            for chunk in range(CHUNKS):
                cols = slice(chunk * LANES, (chunk + 1) * LANES)
                high, low = split(ref[pl.ds(start + chunk, step, stride=ROWS), :])
                xh_ref[rows, cols] = high
                xl_ref[rows, cols] = low
    mixed = dense(xh_ref, xl_ref, high_ref, low_ref)
    for top, bottom, _, start in blocks:
        for chunk in range(CHUNKS):
            cols = slice(chunk * LANES, (chunk + 1) * LANES)
            sine_cols = slice(T + chunk * LANES, T + (chunk + 1) * LANES)
            value = (
                mixed[top, cols] + mixed[bottom, sine_cols],
                mixed[bottom, cols] - mixed[top, sine_cols],
            )
            response = [
                jnp.concatenate(
                    [
                        in_ref[pl.ds(start + b * ROWS + part * CHUNKS + chunk, N_NEAR, stride=SEND_B), :]
                        for b in range(2)
                    ],
                    axis=0,
                )
                for part in range(2)
            ]
            for rows, part in zip((top, bottom), times(value, (response[0] + gain, response[1]))):
                high, low = split(part)
                xh_ref[rows, cols] = high
                xl_ref[rows, cols] = low
    mixed = dense(xh_ref, xl_ref, high_ref, low_ref)
    for top, bottom, start, _ in blocks:
        for chunk in range(CHUNKS):
            cols = slice(chunk * LANES, (chunk + 1) * LANES)
            sine_cols = slice(T + chunk * LANES, T + (chunk + 1) * LANES)
            place = pl.ds(start + chunk, step, stride=ROWS)
            re_ref[place, :] = mixed[top, cols] - mixed[bottom, sine_cols]
            im_ref[place, :] = mixed[bottom, cols] + mixed[top, sine_cols]
    values = []
    for kd in range(D):
        w, b = freq_place(kd)
        at = (b * N_NEAR + w) * ROWS
        value = (re_ref[pl.ds(at, ROWS), :], im_ref[pl.ds(at, ROWS), :])
        values.append(times_conj(value, (turn_ref[kd, 0], turn_ref[kd, 1])))
    values = complex_transform(values, 1)
    scale = jnp.where(packed, 1.0 / FULL, 0.5 / FULL)
    for w in range(N_NEAR):
        for b in range(B):
            d = digit(w, b)
            re, im = times_conj(times_conj(values[d], slow), turned(d))
            summed = jnp.where(upper, re + swap_halves(re), swap_halves(im) - im)
            out_ref[pl.ds(w * SEND_C + b * ROWS, ROWS), :] = (
                jnp.where(packed, re, summed) * scale
            )


def uncoarse_kernel(in_ref, out_ref):
    for b in range(B):
        items = [
            tuple(
                in_ref[pl.ds(i * SEND_C + b * ROWS + part * CHUNKS, CHUNKS), :]
                for part in range(2)
            )
            for i in range(A)
        ]
        freqs = [(items[0][0], None)] + items[1:] + [(items[0][1], None)]
        for a, value in enumerate(real_inverse(freqs)):
            out_ref[pl.ds((a * B + b) * CHUNKS, CHUNKS), :] = value


def gate_kernel(in_ref, q_ref, out_ref):
    for chunk in range(CHUNKS):
        cols = slice(chunk * LANES, (chunk + 1) * LANES)
        gated = q_ref[:, cols].astype(jnp.float32) * in_ref[pl.ds(chunk, N_FAR, stride=CHUNKS), :]
        out_ref[:, cols] = gated.astype(jnp.bfloat16)


def split_table(table):
    high = table.astype(np.float32).astype(ml_dtypes.bfloat16)
    low = (table - high.astype(np.float64)).astype(np.float32).astype(ml_dtypes.bfloat16)
    return high, low


def tables():
    t = np.arange(T)
    angle = 2 * np.pi * (t[:, None] * t[None, :] % T) / T
    high, low = split_table(np.concatenate([np.cos(angle), np.sin(angle)], axis=1))

    def parts(steps, period):
        angles = 2 * np.pi * (steps % period) / period
        return np.stack([np.cos(angles), -np.sin(angles)], axis=-3).astype(np.float32)

    freqs = np.array([item_freqs(i) for i in range(A)])
    slow = parts(freqs[:, :, None] * t, FULL).reshape(A, 2, ROWS, LANES)
    step = 2 * np.pi * (freqs[:, None, :] * np.arange(D)[:, None] % (2 * A * D)) / (2 * A * D)
    step = np.concatenate([np.cos(step), -np.sin(step)], axis=1).transpose(0, 2, 1)
    step = np.repeat(step, CHUNKS, axis=1).astype(np.float32).reshape(A // 2, 2, ROWS, LANES)
    fast = parts(np.arange(D)[:, None, None] * t * np.ones((1, 2, 1), int), D * T)
    return np.concatenate([fast.reshape(D, 2, ROWS, LANES), slow, step]), high, low


VMEM = pl.BlockSpec(memory_space=pltpu.VMEM)
SMEM = pl.BlockSpec(memory_space=pltpu.SMEM)
HBM = pl.BlockSpec(memory_space=pltpu.HBM)


def in_hbm(x):
    return pltpu.with_memory_space_constraint(jnp.asarray(x), pltpu.HBM)


def call(kernel, shape, in_specs, dtype=jnp.float32, scratch=(), limit=VMEM_LIMIT):
    return pl.pallas_call(
        kernel,
        out_shape=jax.ShapeDtypeStruct(shape, dtype),
        in_specs=in_specs,
        out_specs=VMEM,
        scratch_shapes=list(scratch),
        compiler_params=pltpu.CompilerParams(vmem_limit_bytes=limit),
    )


def run_pack(k_proj, v_proj, spectrum):
    return call(
        pack_kernel,
        (N_FAR * SEND_A, LANES),
        [HBM] * 3,
        scratch=[
            pltpu.VMEM(k_proj.shape, k_proj.dtype),
            pltpu.VMEM(v_proj.shape, v_proj.dtype),
            pltpu.VMEM(spectrum.shape, spectrum.dtype),
            pltpu.SemaphoreType.DMA((3,)),
        ],
    )(*(in_hbm(x) for x in (k_proj, v_proj, spectrum)))


def run_coarse(value):
    return call(coarse_kernel, (N_NEAR * SEND_B, LANES), [VMEM])(value)


def run_filter(place, value, gain):
    turns, high, low = tables()
    return call(
        filter_kernel,
        (N_NEAR * SEND_C, LANES),
        [SMEM, VMEM, HBM] + [VMEM] * 3,
        scratch=[pltpu.VMEM((D * ROWS, LANES), jnp.float32)] * 2
        + [pltpu.VMEM((4 * D, T), jnp.bfloat16)] * 2
        + [pltpu.VMEM((1, gain.size), jnp.float32), pltpu.SemaphoreType.DMA],
    )(place, value, in_hbm(gain.reshape(1, -1)), turns, high, low)


def run_uncoarse(value):
    return call(uncoarse_kernel, (N_FAR * CHUNKS, LANES), [VMEM])(value)


def run_gate(value, q_proj):
    return call(gate_kernel, q_proj.shape, [VMEM] * 2, dtype=jnp.bfloat16)(value, q_proj)


def exchange(value, axes, count):
    tile = 8 if value.shape[0] // count % 8 == 0 else 4
    blocks = value.reshape(count, -1, tile, LANES)
    return lax.all_to_all(blocks, axes, 0, 0, tiled=True).reshape(-1, LANES)


def local(q_proj, k_proj, v_proj, skip_gain, spectrum):
    value = run_pack(k_proj, v_proj, spectrum.reshape(4, *k_proj.shape))
    value = exchange(value, FAR, N_FAR)
    value = run_coarse(value)
    value = exchange(value, NEAR, N_NEAR)
    place = jnp.stack([lax.axis_index(FAR), lax.axis_index(NEAR)]).astype(jnp.int32)
    value = run_filter(place, value, skip_gain)
    value = exchange(value, NEAR, N_NEAR)
    value = run_uncoarse(value)
    value = exchange(value, FAR, N_FAR)
    return run_gate(value, q_proj)


def solution(mesh):
    fine = Mesh(mesh.devices.reshape(SIZES), AXES)
    placed = (P(None, AXES), P(None, AXES), P(None, AXES), P(), P(None, None, None, AXES))
    return jax.shard_map(
        local, mesh=fine, in_specs=placed, out_specs=P(None, AXES), check_vma=False
    )
```

time: 99.8 us -> 95.2 us (0.954)
  local copies, waits for them, and re-layouts: 5.07 us -> 0.02 us
  blocking collectives: 68.9 us -> 67 us
  Pallas kernels: 5.27 us -> 6.91 us
  starting transfers between devices: 6.4 us -> 7.51 us
    unnamed x22 -> x8, local copies, waits for them, and re-layouts: 5.07 us -> 0.02 us
    all_to_all x3, blocking collectives: 68.9 us -> 67 us  [exchange(): return lax.all_to_all(blocks, axes, 0, 0, tiled=True).reshape(-1, LANES)]
    all_to_all x1, starting transfers between devices: 6.4 us -> 7.51 us  [exchange(): return lax.all_to_all(blocks, axes, 0, 0, tiled=True).reshape(-1, LANES)]
where the time goes in v4:
time: 95.2 us; the launch traced here: 94.8 us
  blocking collectives  67 us (70%)
  waiting for transfers between devices  13.3 us (14%)
  starting transfers between devices  7.51 us (8%)
  Pallas kernels  6.91 us (7%)
    all_to_all x3, blocking collectives, exchange(): return lax.all_to_all(blocks, axes, 0, 0, tiled=True).reshape(-1, LANES)  67 us
    all_to_all x1, waiting for transfers between devices, exchange(): return lax.all_to_all(blocks, axes, 0, 0, tiled=True).reshape(-1, LANES)  13.3 us
    all_to_all x1, starting transfers between devices, exchange(): return lax.all_to_all(blocks, axes, 0, 0, tiled=True).reshape(-1, LANES)  7.51 us
    pallas_call x1, Pallas kernels, run_filter(): call(filter_kernel, (N_NEAR * SEND_C, LANES), [SMEM, VMEM, HBM] + [VMEM]...  3.99 us
  transfers between devices with their start and end apart: 1, of which 1 were waited for; matrix products, arithmetic and copies ran while one was open for 0% of the time, Pallas kernels for 0%

profile of v4, /device:TPU:1, one launch (start us, length us, event | category | flops | bytes accessed | tf_op | source)
XLA Modules:
  0.0 94.8 jit_solution(15272041972345593095)
XLA Ops:
  0.0 1.2 %shard_map.82 = f32[1280,128]{1,0:T(8,128)S(1)} custom-call(bf16[64,512]{1,0:T(8,128)(2,1)} %k_hbm.1, bf16[64,512]{1,0:T(8,128)(2,1)} %v_hbm.1, f32[4,64,512]{2,1,0:T(8,128)} %bitcast.21), custom_call_target="tpu_custom_call" | custom-call | tf_op jit(solution)/shard_map/pallas_call | solution.py:380
  1.2 39.1 %all_to_all.20 = f32[64,5,4,128]{3,2,1,0:T(4,128)S(1)} all-to-all(f32[64,5,4,128]{3,2,1,0:T(4,128)S(1)} %bitcast.16), channel_id=1, replica_groups=mesh['xl'=2,'yh'=4,'yl'=2,'core'=2,'xh'=2,'zh'=4,'zl'=2] {'xl','yh','yl'..., dimensions={0} | all-to-all | bytes 1310720 | tf_op jit(solution)/shard_map/all_to_all | solution.py:420
  40.3 0.0 copy-start.1
  40.3 0.0 copy-start.2
  40.3 1.0 %shard_map.83 = f32[1536,128]{1,0:T(8,128)} custom-call(f32[1280,128]{1,0:T(8,128)S(1)} %bitcast.15), custom_call_target="tpu_custom_call" | custom-call | tf_op jit(solution)/shard_map/pallas_call | solution.py:394
  41.3 0.0 copy-start
  41.3 7.5 %all-to-all-start.1 = ((f32[8,24,8,128]{3,2,1,0:T(8,128)}), f32[8,24,8,128]{3,2,1,0:T(8,128)S(1)}, u32[]{:S(2)}, u32[]{:S(2)}) async-start(f32[8,24,8,128]{3,2,1,0:T(8,128)} %bitcast.5), calls=%async_computation.1 | async-start | bytes 1572864 | tf_op jit(solution)/shard_map/all_to_all | solution.py:420
  48.9 0.1 pad_add_fusion.place_ref
  48.9 13.3 %all-to-all-done.1 = f32[8,24,8,128]{3,2,1,0:T(8,128)S(1)} async-done(((f32[8,24,8,128]{3,2,1,0:T(8,128)}), f32[8,24,8,128]{3,2,1,0:T(8,128)S(1)}, u32[]{:S(2)}, u32[]{:S(2)}) %all-to-all-start.1) | async-done | bytes 786464 | tf_op jit(solution)/shard_map/all_to_all | solution.py:420
  62.2 0.0 copy-done.1
  62.2 0.0 copy-done.2
  62.2 0.0 copy-done
  62.2 4.0 %shard_map.84 = f32[512,128]{1,0:T(8,128)S(1)} custom-call(s32[2]{0:T(128)S(1)} %pad_add_fusion.place_ref, f32[1536,128]{1,0:T(8,128)S(1)} %bitcast.14, f32[1,64]{1,0:T(1,128)} %bitcast.22, f32[76,2,8,128]{3,2,1,0:T(8,128)S(1)} %copy-done.2, bf16[512,1024]{1,0:T(8,128)(2,1)S(1)} %copy-done.1, bf16[512,1024]{1,0:T(8,128)(2,1)S(1)} %copy-done), custom_call_target="tpu_custom_call" | custom-call | tf_op jit(solution)/shard_map/pallas_call | solution.py:399
  66.2 10.4 %all_to_all.21 = f32[8,8,8,128]{3,2,1,0:T(8,128)S(1)} all-to-all(f32[8,8,8,128]{3,2,1,0:T(8,128)S(1)} %bitcast.17), channel_id=1, replica_groups=mesh['xl'=2,'yh'=4,'yl'=2,'core'=2,'xh'=2,'zh'=4,'zl'=2] {'core','xh','zl'}, dimensions={0} | all-to-all | bytes 524288 | tf_op jit(solution)/shard_map/all_to_all | solution.py:420
  76.6 0.1 shard_map.85
  76.7 0.0 copy-start.3
  76.7 17.5 %all_to_all.22 = f32[64,1,4,128]{3,2,1,0:T(4,128)S(1)} all-to-all(f32[64,1,4,128]{3,2,1,0:T(4,128)S(1)} %bitcast.19), channel_id=1, replica_groups=mesh['xl'=2,'yh'=4,'yl'=2,'core'=2,'xh'=2,'zh'=4,'zl'=2] {'xl','yh','yl'..., dimensions={0} | all-to-all | bytes 262144 | tf_op jit(solution)/shard_map/all_to_all | solution.py:420
  94.2 0.0 copy-done.3
  94.2 0.6 shard_map.86
Async XLA Ops:
  40.3 21.9 %copy-start.1 = (bf16[512,1024]{1,0:T(8,128)(2,1)S(1)}, bf16[512,1024]{1,0:T(8,128)(2,1)}, u32[]{:S(2)}) copy-start(bf16[512,1024]{1,0:T(8,128)(2,1)} %constant.42.clone.high_ref) | copy-start | bytes 3145732
  40.3 21.9 %copy-start.2 = (f32[76,2,8,128]{3,2,1,0:T(8,128)S(1)}, f32[76,2,8,128]{3,2,1,0:T(8,128)}, u32[]{:S(2)}) copy-start(f32[76,2,8,128]{3,2,1,0:T(8,128)} %constant.41.clone.turn_ref) | copy-start | bytes 1867780
  41.3 20.9 %copy-start = (bf16[512,1024]{1,0:T(8,128)(2,1)S(1)}, bf16[512,1024]{1,0:T(8,128)(2,1)}, u32[]{:S(2)}) copy-start(bf16[512,1024]{1,0:T(8,128)(2,1)} %constant.43.clone.low_ref) | copy-start | bytes 3145732
  41.3 20.9 %all-to-all-start.1 = ((f32[8,24,8,128]{3,2,1,0:T(8,128)}), f32[8,24,8,128]{3,2,1,0:T(8,128)S(1)}, u32[]{:S(2)}, u32[]{:S(2)}) async-start(f32[8,24,8,128]{3,2,1,0:T(8,128)} %bitcast.5), calls=%async_computation.1 | async-start | bytes 1572864 | tf_op jit(solution)/shard_map/all_to_all | solution.py:420
  76.7 17.5 %copy-start.3 = (bf16[64,512]{1,0:T(8,128)(2,1)S(1)}, bf16[64,512]{1,0:T(8,128)(2,1)}, u32[]{:S(2)}) copy-start(bf16[64,512]{1,0:T(8,128)(2,1)} %q_ref.1) | copy-start | bytes 196612

commit v5 on v4

--- a/solution.py
+++ b/solution.py
@@ -421,11 +421,12 @@
 
 
 def local(q_proj, k_proj, v_proj, skip_gain, spectrum):
+    place = jnp.stack([lax.axis_index(FAR), lax.axis_index(NEAR)]).astype(jnp.int32)
     value = run_pack(k_proj, v_proj, spectrum.reshape(4, *k_proj.shape))
+    value, place = lax.optimization_barrier((value, place))
     value = exchange(value, FAR, N_FAR)
     value = run_coarse(value)
     value = exchange(value, NEAR, N_NEAR)
-    place = jnp.stack([lax.axis_index(FAR), lax.axis_index(NEAR)]).astype(jnp.int32)
     value = run_filter(place, value, skip_gain)
     value = exchange(value, NEAR, N_NEAR)
     value = run_uncoarse(value)

time: 95.2 us -> 94.3 us (level)
  blocking collectives: 67 us -> 87.8 us
  waiting for transfers between devices: 13.3 us -> 0 us
  starting transfers between devices: 7.51 us -> 0 us
    all_to_all x3 -> x4, blocking collectives: 67 us -> 87.8 us  [exchange(): return lax.all_to_all(blocks, axes, 0, 0, tiled=True).reshape(-1, LANES)]
    all_to_all x1 -> x0, waiting for transfers between devices: 13.3 us -> none  [exchange(): return lax.all_to_all(blocks, axes, 0, 0, tiled=True).reshape(-1, LANES)]
    all_to_all x1 -> x0, starting transfers between devices: 7.51 us -> none  [exchange(): return lax.all_to_all(blocks, axes, 0, 0, tiled=True).reshape(-1, LANES)]
  transfers between devices with their start and end apart: 1 -> 0, of which waited for: 1 -> 0; matrix products, arithmetic and copies ran while one was open for 0% -> 0% of each run, Pallas kernels for 0% -> 0%
where the time goes in v5:
time: 94.3 us; the launch traced here: 94 us
  blocking collectives  87.8 us (93%)
  Pallas kernels  6.09 us (6%)
    all_to_all x4, blocking collectives, exchange(): return lax.all_to_all(blocks, axes, 0, 0, tiled=True).reshape(-1, LANES)  87.8 us
    pallas_call x1, Pallas kernels, run_filter(): call(filter_kernel, (N_NEAR * SEND_C, LANES), [SMEM, VMEM, HBM] + [VMEM]...  4.07 us

profile of v5, /device:TPU:1, one launch (start us, length us, event | category | flops | bytes accessed | tf_op | source)
XLA Modules:
  0.0 94.0 jit_solution(7625892158144804827)
XLA Ops:
  0.0 0.1 pad_add_fusion.place_ref
  0.1 1.2 %shard_map.82 = f32[1280,128]{1,0:T(8,128)S(1)} custom-call(bf16[64,512]{1,0:T(8,128)(2,1)} %k_hbm.1, bf16[64,512]{1,0:T(8,128)(2,1)} %v_hbm.1, f32[4,64,512]{2,1,0:T(8,128)} %bitcast.22), custom_call_target="tpu_custom_call" | custom-call | tf_op jit(solution)/shard_map/pallas_call | solution.py:380
  1.3 39.1 %all_to_all.20 = f32[64,5,4,128]{3,2,1,0:T(4,128)S(1)} all-to-all(f32[64,5,4,128]{3,2,1,0:T(4,128)S(1)} %bitcast.17), channel_id=1, replica_groups=mesh['xl'=2,'yh'=4,'yl'=2,'core'=2,'xh'=2,'zh'=4,'zl'=2] {'xl','yh','yl'..., dimensions={0} | all-to-all | bytes 1310720 | tf_op jit(solution)/shard_map/all_to_all | solution.py:420
  40.4 0.0 copy-start.1
  40.4 0.0 copy-start.2
  40.4 0.1 shard_map.83
  40.5 0.0 copy-start
  40.5 20.7 %all_to_all.21 = f32[8,24,8,128]{3,2,1,0:T(8,128)S(1)} all-to-all(f32[8,24,8,128]{3,2,1,0:T(8,128)S(1)} %bitcast.15), channel_id=1, replica_groups=mesh['xl'=2,'yh'=4,'yl'=2,'core'=2,'xh'=2,'zh'=4,'zl'=2] {'core','xh','zl'}, dimensions={0} | all-to-all | bytes 1572864 | tf_op jit(solution)/shard_map/all_to_all | solution.py:420
  61.2 0.0 copy-done.1
  61.2 0.0 copy-done.2
  61.2 0.0 copy-done
  61.2 4.1 %shard_map.84 = f32[512,128]{1,0:T(8,128)S(1)} custom-call(s32[2]{0:T(128)S(1)} %pad_add_fusion.place_ref, f32[1536,128]{1,0:T(8,128)S(1)} %bitcast.14, f32[1,64]{1,0:T(1,128)} %bitcast.23, f32[76,2,8,128]{3,2,1,0:T(8,128)S(1)} %copy-done.2, bf16[512,1024]{1,0:T(8,128)(2,1)S(1)} %copy-done.1, bf16[512,1024]{1,0:T(8,128)(2,1)S(1)} %copy-done), custom_call_target="tpu_custom_call" | custom-call | tf_op jit(solution)/shard_map/pallas_call | solution.py:399
  65.3 10.5 %all_to_all.22 = f32[8,8,8,128]{3,2,1,0:T(8,128)S(1)} all-to-all(f32[8,8,8,128]{3,2,1,0:T(8,128)S(1)} %bitcast.18), channel_id=1, replica_groups=mesh['xl'=2,'yh'=4,'yl'=2,'core'=2,'xh'=2,'zh'=4,'zl'=2] {'core','xh','zl'}, dimensions={0} | all-to-all | bytes 524288 | tf_op jit(solution)/shard_map/all_to_all | solution.py:420
  75.8 0.1 shard_map.85
  75.9 0.0 copy-start.3
  75.9 17.5 %all_to_all.23 = f32[64,1,4,128]{3,2,1,0:T(4,128)S(1)} all-to-all(f32[64,1,4,128]{3,2,1,0:T(4,128)S(1)} %bitcast.20), channel_id=1, replica_groups=mesh['xl'=2,'yh'=4,'yl'=2,'core'=2,'xh'=2,'zh'=4,'zl'=2] {'xl','yh','yl'..., dimensions={0} | all-to-all | bytes 262144 | tf_op jit(solution)/shard_map/all_to_all | solution.py:420
  93.4 0.0 copy-done.3
  93.4 0.6 shard_map.86
Async XLA Ops:
  40.4 20.8 %copy-start.1 = (bf16[512,1024]{1,0:T(8,128)(2,1)S(1)}, bf16[512,1024]{1,0:T(8,128)(2,1)}, u32[]{:S(2)}) copy-start(bf16[512,1024]{1,0:T(8,128)(2,1)} %constant.42.clone.high_ref) | copy-start | bytes 3145732
  40.4 20.8 %copy-start.2 = (f32[76,2,8,128]{3,2,1,0:T(8,128)S(1)}, f32[76,2,8,128]{3,2,1,0:T(8,128)}, u32[]{:S(2)}) copy-start(f32[76,2,8,128]{3,2,1,0:T(8,128)} %constant.41.clone.turn_ref) | copy-start | bytes 1867780
  40.5 20.7 %copy-start = (bf16[512,1024]{1,0:T(8,128)(2,1)S(1)}, bf16[512,1024]{1,0:T(8,128)(2,1)}, u32[]{:S(2)}) copy-start(bf16[512,1024]{1,0:T(8,128)(2,1)} %constant.43.clone.low_ref) | copy-start | bytes 3145732
  75.9 17.5 %copy-start.3 = (bf16[64,512]{1,0:T(8,128)(2,1)S(1)}, bf16[64,512]{1,0:T(8,128)(2,1)}, u32[]{:S(2)}) copy-start(bf16[64,512]{1,0:T(8,128)(2,1)} %q_ref.1) | copy-start | bytes 196612

commit v6 on v4

--- a/solution.py
+++ b/solution.py
@@ -11,8 +11,8 @@
 
 AXES = ("xl", "yh", "yl", "core", "xh", "zh", "zl")
 SIZES = (2, 4, 2, 2, 2, 4, 2)
-FAR = ("xl", "yh", "yl", "zh")
-NEAR = ("core", "xh", "zl")
+FAR = ("xl", "yh", "zh", "zl")
+NEAR = ("yl", "core", "xh")
 A = 8
 B = 8
 N_FAR = A * B
@@ -23,7 +23,7 @@
 CHUNKS = T // LANES
 ROWS = 2 * CHUNKS
 FULL = 2 * A * D * T
-VMEM_LIMIT = 12 * 1024 * 1024
+VMEM_LIMIT = 24 * 1024 * 1024
 
 
 def item_freqs(i):
@@ -36,14 +36,12 @@
 
 
 def digit(w, b):
-    core, xh, zl = w >> 2, w >> 1 & 1, w & 1
-    yl, zh = b >> 2, b & 3
-    return yl * 32 + core * 16 + xh * 8 + zh * 2 + zl
+    return w * 8 + b
 
 
 def freq_place(kd):
     y0, core, z0, z1, z2, xh = (kd >> bit & 1 for bit in range(6))
-    return core * 4 + xh * 2 + z0, y0 * 4 + z2 * 2 + z1
+    return y0 * 4 + core * 2 + xh, z2 * 4 + z1 * 2 + z0
 
 
 def add(a, b):
@@ -144,13 +142,16 @@
 SEND_A = 5 * CHUNKS
 SEND_B = 3 * B * ROWS
 SEND_C = B * ROWS
-
-
-def pack_kernel(k_hbm, v_hbm, spec_hbm, out_ref, k_ref, v_ref, spec_ref, sems):
+PITCH = (2 * B + 1) * ROWS
+
+
+def pack_kernel(
+    k_hbm, v_hbm, gain_hbm, spec_hbm, out_ref, k_ref, v_ref, gain_ref, spec_ref, sems
+):
     copies = [
         pltpu.make_async_copy(source, target, sems.at[i])
         for i, (source, target) in enumerate(
-            ((k_hbm, k_ref), (v_hbm, v_ref), (spec_hbm, spec_ref))
+            ((k_hbm, k_ref), (v_hbm, v_ref), (gain_hbm, gain_ref), (spec_hbm, spec_ref))
         )
     ]
     for copy in copies:
@@ -162,11 +163,18 @@
         cols = slice(chunk * LANES, (chunk + 1) * LANES)
         out_ref[pl.ds(chunk, N_FAR, stride=SEND_A), :] = product[:, cols]
     copies[2].wait()
+    row = lax.broadcasted_iota(jnp.int32, (N_FAR, N_FAR), 0)
+    col = lax.broadcasted_iota(jnp.int32, (N_FAR, N_FAR), 1)
+    spread = jnp.broadcast_to(gain_ref[...], (N_FAR, N_FAR))
+    gain = jnp.sum(jnp.where(row == col, spread, 0.0), axis=1, keepdims=True)
+    copies[3].wait()
     for part in range(4):
         for chunk in range(CHUNKS):
             cols = slice(chunk * LANES, (chunk + 1) * LANES)
             place = (1 + part) * CHUNKS + chunk
-            out_ref[pl.ds(place, N_FAR, stride=SEND_A), :] = spec_ref[part, :, cols]
+            value = spec_ref[part, :, cols]
+            value = value + gain if part % 2 == 0 else value
+            out_ref[pl.ds(place, N_FAR, stride=SEND_A), :] = value
 
 
 def coarse_kernel(in_ref, out_ref):
@@ -206,13 +214,16 @@
 
 
 def filter_kernel(
-    place_ref, in_ref, gain_hbm, turn_ref, high_ref, low_ref, out_ref,
-    re_ref, im_ref, xh_ref, xl_ref, gain_ref, sem,
+    item_ref, in_ref, turn_ref, high_ref, low_ref, out_ref,
+    re_ref, im_ref, xh_ref, xl_ref, response_ref,
 ):
-    gain_copy = pltpu.make_async_copy(gain_hbm, gain_ref, sem)
-    gain_copy.start()
-    channel, item = place_ref[0], place_ref[1]
+    item = item_ref[0]
     packed = item == 0
+    for w in range(N_NEAR):
+        for at in range(2 * B):
+            response_ref[pl.ds(w * PITCH + at * ROWS, ROWS), :] = in_ref[
+                pl.ds(w * SEND_B + (B + at) * ROWS, ROWS), :
+            ]
     upper = upper_rows()
     keep = jnp.logical_or(upper, packed)
     signs = jnp.where(upper, 1.0, -1.0) * jnp.where(packed, 0.0, 1.0)
@@ -238,9 +249,6 @@
         re_ref[pl.ds(at, ROWS), :], im_ref[pl.ds(at, ROWS), :] = times(
             value, (turn_ref[kd, 0], turn_ref[kd, 1])
         )
-    gain_copy.wait()
-    lane = lax.broadcasted_iota(jnp.int32, gain_ref.shape, 1)
-    gain = jnp.sum(jnp.where(lane == channel, gain_ref[...], 0.0))
     half_rows = 2 * D
     step = 2 * N_NEAR
     blocks = []
@@ -252,7 +260,7 @@
                     slice(first, first + step),
                     slice(half_rows + first, half_rows + first + step),
                     b * N_NEAR * ROWS + side * CHUNKS,
-                    (B + side * B + b) * ROWS,
+                    (side * B + b) * ROWS,
                 )
             )
     for top, bottom, start, _ in blocks:
@@ -274,14 +282,14 @@
             response = [
                 jnp.concatenate(
                     [
-                        in_ref[pl.ds(start + b * ROWS + part * CHUNKS + chunk, N_NEAR, stride=SEND_B), :]
+                        response_ref[pl.ds(start + b * ROWS + part * CHUNKS + chunk, N_NEAR, stride=PITCH), :]
                         for b in range(2)
                     ],
                     axis=0,
                 )
                 for part in range(2)
             ]
-            for rows, part in zip((top, bottom), times(value, (response[0] + gain, response[1]))):
+            for rows, part in zip((top, bottom), times(value, response)):
                 high, low = split(part)
                 xh_ref[rows, cols] = high
                 xl_ref[rows, cols] = low
@@ -376,34 +384,33 @@
     )
 
 
-def run_pack(k_proj, v_proj, spectrum):
+def run_pack(k_proj, v_proj, gain, spectrum):
+    operands = (k_proj, v_proj, gain.reshape(1, -1), spectrum.reshape(4, *k_proj.shape))
     return call(
         pack_kernel,
         (N_FAR * SEND_A, LANES),
-        [HBM] * 3,
-        scratch=[
-            pltpu.VMEM(k_proj.shape, k_proj.dtype),
-            pltpu.VMEM(v_proj.shape, v_proj.dtype),
-            pltpu.VMEM(spectrum.shape, spectrum.dtype),
-            pltpu.SemaphoreType.DMA((3,)),
-        ],
-    )(*(in_hbm(x) for x in (k_proj, v_proj, spectrum)))
+        [HBM] * 4,
+        scratch=[pltpu.VMEM(x.shape, x.dtype) for x in operands]
+        + [pltpu.SemaphoreType.DMA((4,))],
+    )(*(in_hbm(x) for x in operands))
 
 
 def run_coarse(value):
     return call(coarse_kernel, (N_NEAR * SEND_B, LANES), [VMEM])(value)
 
 
-def run_filter(place, value, gain):
+def run_filter(item, value):
     turns, high, low = tables()
     return call(
         filter_kernel,
         (N_NEAR * SEND_C, LANES),
-        [SMEM, VMEM, HBM] + [VMEM] * 3,
+        [SMEM] + [VMEM] * 4,
         scratch=[pltpu.VMEM((D * ROWS, LANES), jnp.float32)] * 2
         + [pltpu.VMEM((4 * D, T), jnp.bfloat16)] * 2
-        + [pltpu.VMEM((1, gain.size), jnp.float32), pltpu.SemaphoreType.DMA],
-    )(place, value, in_hbm(gain.reshape(1, -1)), turns, high, low)
+        + [
+            pltpu.VMEM((N_NEAR * PITCH, LANES), jnp.float32),
+        ],
+    )(item, value, turns, high, low)
 
 
 def run_uncoarse(value):
@@ -421,12 +428,13 @@
 
 
 def local(q_proj, k_proj, v_proj, skip_gain, spectrum):
-    value = run_pack(k_proj, v_proj, spectrum.reshape(4, *k_proj.shape))
+    item = lax.axis_index(NEAR).astype(jnp.int32).reshape(1)
+    value = run_pack(k_proj, v_proj, skip_gain, spectrum)
+    value, item = lax.optimization_barrier((value, item))
     value = exchange(value, FAR, N_FAR)
     value = run_coarse(value)
     value = exchange(value, NEAR, N_NEAR)
-    place = jnp.stack([lax.axis_index(FAR), lax.axis_index(NEAR)]).astype(jnp.int32)
-    value = run_filter(place, value, skip_gain)
+    value = run_filter(item, value)
     value = exchange(value, NEAR, N_NEAR)
     value = run_uncoarse(value)
     value = exchange(value, FAR, N_FAR)

time: 95.2 us -> 92.9 us (0.976)
  blocking collectives: 67 us -> 87.1 us
  waiting for transfers between devices: 13.3 us -> 0 us
  starting transfers between devices: 7.51 us -> 0 us
  Pallas kernels: 6.91 us -> 5.2 us
    all_to_all x3 -> x4, blocking collectives: 67 us -> 87.1 us  [exchange(): return lax.all_to_all(blocks, axes, 0, 0, tiled=True).reshape(-1, LANES)]
    all_to_all x1 -> x0, waiting for transfers between devices: 13.3 us -> none  [exchange(): return lax.all_to_all(blocks, axes, 0, 0, tiled=True).reshape(-1, LANES)]
    all_to_all x1 -> x0, starting transfers between devices: 7.51 us -> none  [exchange(): return lax.all_to_all(blocks, axes, 0, 0, tiled=True).reshape(-1, LANES)]
  transfers between devices with their start and end apart: 1 -> 0, of which waited for: 1 -> 0; matrix products, arithmetic and copies ran while one was open for 0% -> 0% of each run, Pallas kernels for 0% -> 0%
where the time goes in v6:
time: 92.9 us; the launch traced here: 92.4 us
  blocking collectives  87.1 us (94%)
  Pallas kernels  5.2 us (6%)
    all_to_all x4, blocking collectives, exchange(): return lax.all_to_all(blocks, axes, 0, 0, tiled=True).reshape(-1, LANES)  87.1 us
    pallas_call x1, Pallas kernels, run_filter(): call(filter_kernel, (N_NEAR * SEND_C, LANES), [SMEM] + [VMEM] * 4, scratc...  3.15 us

profile of v6, /device:TPU:1, one launch (start us, length us, event | category | flops | bytes accessed | tf_op | source)
XLA Modules:
  0.0 92.4 jit_solution(17803583019207216117)
XLA Ops:
  0.0 1.2 %shard_map.82 = f32[1280,128]{1,0:T(8,128)S(1)} custom-call(bf16[64,512]{1,0:T(8,128)(2,1)} %k_hbm.1, bf16[64,512]{1,0:T(8,128)(2,1)} %v_hbm.1, f32[1,64]{1,0:T(1,128)} %bitcast.22, f32[4,64,512]{2,1,0:T(8,128)} %bitcast.21), custom_call_target="tpu_custom_call" | custom-call | tf_op jit(solution)/shard_map/pallas_call | solution.py:389
  1.2 40.4 %all_to_all.20 = f32[64,5,4,128]{3,2,1,0:T(4,128)S(1)} all-to-all(f32[64,5,4,128]{3,2,1,0:T(4,128)S(1)} %bitcast.16), channel_id=1, replica_groups=mesh['xl'=2,'yh'=4,'yl'=2,'core'=2,'xh'=2,'zh'=4,'zl'=2] {'xl','yh','zh'..., dimensions={0} | all-to-all | bytes 1310720 | tf_op jit(solution)/shard_map/all_to_all | solution.py:427
  41.6 0.0 copy-start.1
  41.6 0.0 copy-start.2
  41.6 0.1 shard_map.83
  41.7 0.0 copy-start
  41.7 18.8 %all_to_all.21 = f32[8,24,8,128]{3,2,1,0:T(8,128)S(1)} all-to-all(f32[8,24,8,128]{3,2,1,0:T(8,128)S(1)} %bitcast.13), channel_id=1, replica_groups=mesh['xl'=2,'yh'=4,'yl'=2,'core'=2,'xh'=2,'zh'=4,'zl'=2] {'yl','core','xh'}, dimensions={0} | all-to-all | bytes 1572864 | tf_op jit(solution)/shard_map/all_to_all | solution.py:427
  60.5 0.0 copy-done.1
  60.5 0.0 copy-done.2
  60.5 0.0 copy-done
  60.5 3.1 %shard_map.84 = f32[512,128]{1,0:T(8,128)S(1)} custom-call(s32[1]{0:T(128)} %bitcast.2.item_ref, f32[1536,128]{1,0:T(8,128)S(1)} %bitcast.14, f32[76,2,8,128]{3,2,1,0:T(8,128)S(1)} %copy-done.2, bf16[512,1024]{1,0:T(8,128)(2,1)S(1)} %copy-done.1, bf16[512,1024]{1,0:T(8,128)(2,1)S(1)} %copy-done), custom_call_target="tpu_custom_call" | custom-call | tf_op jit(solution)/shard_map/pallas_call | solution.py:404
  63.7 10.1 %all_to_all.22 = f32[8,8,8,128]{3,2,1,0:T(8,128)S(1)} all-to-all(f32[8,8,8,128]{3,2,1,0:T(8,128)S(1)} %bitcast.17), channel_id=1, replica_groups=mesh['xl'=2,'yh'=4,'yl'=2,'core'=2,'xh'=2,'zh'=4,'zl'=2] {'yl','core','xh'}, dimensions={0} | all-to-all | bytes 524288 | tf_op jit(solution)/shard_map/all_to_all | solution.py:427
  73.8 0.1 shard_map.85
  73.9 0.0 copy-start.3
  73.9 17.8 %all_to_all.23 = f32[64,1,4,128]{3,2,1,0:T(4,128)S(1)} all-to-all(f32[64,1,4,128]{3,2,1,0:T(4,128)S(1)} %bitcast.19), channel_id=1, replica_groups=mesh['xl'=2,'yh'=4,'yl'=2,'core'=2,'xh'=2,'zh'=4,'zl'=2] {'xl','yh','zh'..., dimensions={0} | all-to-all | bytes 262144 | tf_op jit(solution)/shard_map/all_to_all | solution.py:427
  91.7 0.0 copy-done.3
  91.7 0.6 shard_map.86
Async XLA Ops:
  41.6 18.9 %copy-start.1 = (bf16[512,1024]{1,0:T(8,128)(2,1)S(1)}, bf16[512,1024]{1,0:T(8,128)(2,1)}, u32[]{:S(2)}) copy-start(bf16[512,1024]{1,0:T(8,128)(2,1)} %constant.25.clone.high_ref) | copy-start | bytes 3145732
  41.6 18.9 %copy-start.2 = (f32[76,2,8,128]{3,2,1,0:T(8,128)S(1)}, f32[76,2,8,128]{3,2,1,0:T(8,128)}, u32[]{:S(2)}) copy-start(f32[76,2,8,128]{3,2,1,0:T(8,128)} %constant.24.clone.turn_ref) | copy-start | bytes 1867780
  41.7 18.8 %copy-start = (bf16[512,1024]{1,0:T(8,128)(2,1)S(1)}, bf16[512,1024]{1,0:T(8,128)(2,1)}, u32[]{:S(2)}) copy-start(bf16[512,1024]{1,0:T(8,128)(2,1)} %constant.26.clone.low_ref) | copy-start | bytes 3145732
  73.9 17.9 %copy-start.3 = (bf16[64,512]{1,0:T(8,128)(2,1)S(1)}, bf16[64,512]{1,0:T(8,128)(2,1)}, u32[]{:S(2)}) copy-start(bf16[64,512]{1,0:T(8,128)(2,1)} %q_ref.1) | copy-start | bytes 196612

commit v7 on v6

--- a/solution.py
+++ b/solution.py
@@ -206,16 +206,17 @@
     return high, (value - high.astype(jnp.float32)).astype(jnp.bfloat16)
 
 
-def dense(xh_ref, xl_ref, high_ref, low_ref):
+def dense(x_ref, high_ref, low_ref):
     def dot(a, b):
-        return jnp.dot(a[...], b[...], preferred_element_type=jnp.float32)
-
-    return dot(xh_ref, high_ref) + (dot(xl_ref, high_ref) + dot(xh_ref, low_ref))
+        return jnp.dot(a, b[...], preferred_element_type=jnp.float32)
+
+    both = dot(x_ref[...], high_ref)
+    return both[: 4 * D] + (both[4 * D :] + dot(x_ref[: 4 * D, :], low_ref))
 
 
 def filter_kernel(
     item_ref, in_ref, turn_ref, high_ref, low_ref, out_ref,
-    re_ref, im_ref, xh_ref, xl_ref, response_ref,
+    re_ref, im_ref, x_ref, response_ref,
 ):
     item = item_ref[0]
     packed = item == 0
@@ -268,9 +269,9 @@
             for chunk in range(CHUNKS):
                 cols = slice(chunk * LANES, (chunk + 1) * LANES)
                 high, low = split(ref[pl.ds(start + chunk, step, stride=ROWS), :])
-                xh_ref[rows, cols] = high
-                xl_ref[rows, cols] = low
-    mixed = dense(xh_ref, xl_ref, high_ref, low_ref)
+                x_ref[rows, cols] = high
+                x_ref[slice(rows.start + 4 * D, rows.stop + 4 * D), cols] = low
+    mixed = dense(x_ref, high_ref, low_ref)
     for top, bottom, _, start in blocks:
         for chunk in range(CHUNKS):
             cols = slice(chunk * LANES, (chunk + 1) * LANES)
@@ -291,9 +292,9 @@
             ]
             for rows, part in zip((top, bottom), times(value, response)):
                 high, low = split(part)
-                xh_ref[rows, cols] = high
-                xl_ref[rows, cols] = low
-    mixed = dense(xh_ref, xl_ref, high_ref, low_ref)
+                x_ref[rows, cols] = high
+                x_ref[slice(rows.start + 4 * D, rows.stop + 4 * D), cols] = low
+    mixed = dense(x_ref, high_ref, low_ref)
     for top, bottom, start, _ in blocks:
         for chunk in range(CHUNKS):
             cols = slice(chunk * LANES, (chunk + 1) * LANES)
@@ -406,8 +407,8 @@
         (N_NEAR * SEND_C, LANES),
         [SMEM] + [VMEM] * 4,
         scratch=[pltpu.VMEM((D * ROWS, LANES), jnp.float32)] * 2
-        + [pltpu.VMEM((4 * D, T), jnp.bfloat16)] * 2
         + [
+            pltpu.VMEM((8 * D, T), jnp.bfloat16),
             pltpu.VMEM((N_NEAR * PITCH, LANES), jnp.float32),
         ],
     )(item, value, turns, high, low)

time: 92.9 us -> 92.9 us (level)
  no operation moved by 1% of the time
where the time goes in v7:
time: 92.9 us; the launch traced here: 92.3 us
  blocking collectives  87.1 us (94%)
  Pallas kernels  5.14 us (6%)
    all_to_all x4, blocking collectives, exchange(): return lax.all_to_all(blocks, axes, 0, 0, tiled=True).reshape(-1, LANES)  87.1 us
    pallas_call x1, Pallas kernels, run_filter(): call(filter_kernel, (N_NEAR * SEND_C, LANES), [SMEM] + [VMEM] * 4, scratc...  3.09 us

profile of v7, /device:TPU:1, one launch (start us, length us, event | category | flops | bytes accessed | tf_op | source)
XLA Modules:
  0.0 92.3 jit_solution(853884785557825977)
XLA Ops:
  0.0 1.2 %shard_map.82 = f32[1280,128]{1,0:T(8,128)S(1)} custom-call(bf16[64,512]{1,0:T(8,128)(2,1)} %k_hbm.1, bf16[64,512]{1,0:T(8,128)(2,1)} %v_hbm.1, f32[1,64]{1,0:T(1,128)} %bitcast.22, f32[4,64,512]{2,1,0:T(8,128)} %bitcast.21), custom_call_target="tpu_custom_call" | custom-call | tf_op jit(solution)/shard_map/pallas_call | solution.py:390
  1.2 40.4 %all_to_all.20 = f32[64,5,4,128]{3,2,1,0:T(4,128)S(1)} all-to-all(f32[64,5,4,128]{3,2,1,0:T(4,128)S(1)} %bitcast.16), channel_id=1, replica_groups=mesh['xl'=2,'yh'=4,'yl'=2,'core'=2,'xh'=2,'zh'=4,'zl'=2] {'xl','yh','zh'..., dimensions={0} | all-to-all | bytes 1310720 | tf_op jit(solution)/shard_map/all_to_all | solution.py:428
  41.6 0.0 copy-start.1
  41.6 0.0 copy-start.2
  41.6 0.1 shard_map.83
  41.7 0.0 copy-start
  41.7 18.8 %all_to_all.21 = f32[8,24,8,128]{3,2,1,0:T(8,128)S(1)} all-to-all(f32[8,24,8,128]{3,2,1,0:T(8,128)S(1)} %bitcast.13), channel_id=1, replica_groups=mesh['xl'=2,'yh'=4,'yl'=2,'core'=2,'xh'=2,'zh'=4,'zl'=2] {'yl','core','xh'}, dimensions={0} | all-to-all | bytes 1572864 | tf_op jit(solution)/shard_map/all_to_all | solution.py:428
  60.5 0.0 copy-done.1
  60.5 0.0 copy-done.2
  60.5 0.0 copy-done
  60.5 3.1 %shard_map.84 = f32[512,128]{1,0:T(8,128)S(1)} custom-call(s32[1]{0:T(128)} %bitcast.2.item_ref, f32[1536,128]{1,0:T(8,128)S(1)} %bitcast.14, f32[76,2,8,128]{3,2,1,0:T(8,128)S(1)} %copy-done.2, bf16[512,1024]{1,0:T(8,128)(2,1)S(1)} %copy-done.1, bf16[512,1024]{1,0:T(8,128)(2,1)S(1)} %copy-done), custom_call_target="tpu_custom_call" | custom-call | tf_op jit(solution)/shard_map/pallas_call | solution.py:405
  63.6 10.1 %all_to_all.22 = f32[8,8,8,128]{3,2,1,0:T(8,128)S(1)} all-to-all(f32[8,8,8,128]{3,2,1,0:T(8,128)S(1)} %bitcast.17), channel_id=1, replica_groups=mesh['xl'=2,'yh'=4,'yl'=2,'core'=2,'xh'=2,'zh'=4,'zl'=2] {'yl','core','xh'}, dimensions={0} | all-to-all | bytes 524288 | tf_op jit(solution)/shard_map/all_to_all | solution.py:428
  73.7 0.1 shard_map.85
  73.8 0.0 copy-start.3
  73.8 17.8 %all_to_all.23 = f32[64,1,4,128]{3,2,1,0:T(4,128)S(1)} all-to-all(f32[64,1,4,128]{3,2,1,0:T(4,128)S(1)} %bitcast.19), channel_id=1, replica_groups=mesh['xl'=2,'yh'=4,'yl'=2,'core'=2,'xh'=2,'zh'=4,'zl'=2] {'xl','yh','zh'..., dimensions={0} | all-to-all | bytes 262144 | tf_op jit(solution)/shard_map/all_to_all | solution.py:428
  91.7 0.0 copy-done.3
  91.7 0.6 shard_map.86
Async XLA Ops:
  41.6 18.9 %copy-start.1 = (bf16[512,1024]{1,0:T(8,128)(2,1)S(1)}, bf16[512,1024]{1,0:T(8,128)(2,1)}, u32[]{:S(2)}) copy-start(bf16[512,1024]{1,0:T(8,128)(2,1)} %constant.25.clone.high_ref) | copy-start | bytes 3145732
  41.6 18.9 %copy-start.2 = (f32[76,2,8,128]{3,2,1,0:T(8,128)S(1)}, f32[76,2,8,128]{3,2,1,0:T(8,128)}, u32[]{:S(2)}) copy-start(f32[76,2,8,128]{3,2,1,0:T(8,128)} %constant.24.clone.turn_ref) | copy-start | bytes 1867780
  41.7 18.8 %copy-start = (bf16[512,1024]{1,0:T(8,128)(2,1)S(1)}, bf16[512,1024]{1,0:T(8,128)(2,1)}, u32[]{:S(2)}) copy-start(bf16[512,1024]{1,0:T(8,128)(2,1)} %constant.26.clone.low_ref) | copy-start | bytes 3145732
  73.8 17.9 %copy-start.3 = (bf16[64,512]{1,0:T(8,128)(2,1)S(1)}, bf16[64,512]{1,0:T(8,128)(2,1)}, u32[]{:S(2)}) copy-start(bf16[64,512]{1,0:T(8,128)(2,1)} %q_ref.1) | copy-start | bytes 196612
